TPU v7x, 256 devices: a whole 4x4x8 slice. The times are simulated.
256 devices in a mesh: sect: 2 (over z_lo), grp: 64 (over y, z_hi, x), tp: 2 (over core).
Axes of the slice: x: 4, y: 4, z: 8 (z_hi: 4, z_lo: 2; z = z_hi * 2 + z_lo), core: 2. Of those that a mesh axis runs over, the one named last changes fastest.
Arguments:
- queries: bfloat16 [2, 512, 128, 576], P('sect', 'grp', 'tp'), may hold values from -11 to 11
- latent_rotary_cache: bfloat16 [2, 512, 512, 576], P('sect', 'grp'), may hold values from -4 to 4
- lengths: int32 [2, 512], P('sect', 'grp'), may hold values from 2 to 512, as said below
- section_hidden_rows: bfloat16 [2, 512, 7168], P('sect', 'grp', 'tp'), may hold values from -6 to 6
- row_expert_index: int32 [2, 512, 8], P('sect', 'grp'), may hold values from 0 to 15, all different within a row; in each aligned block of 8 rows (0 to 7, 8 to 15, ..., all dimensions but the last counted through in order) at most 8 rows name the same one
- routing_gate_weight: float32 [2, 512, 8], P('sect', 'grp'), may hold values from 0.05 to 0.5
- gate_matrix: bfloat16 [2, 7168, 16384], P('sect', 'tp', 'grp'), may hold values from -0.0625 to 0.0625
- up_weight: bfloat16 [2, 7168, 16384], P('sect', 'tp', 'grp'), may hold values from -0.0625 to 0.0625
- down_weight: bfloat16 [2, 16384, 7168], P('sect', 'grp', 'tp'), may hold values from -0.1875 to 0.1875
- adapter_input_factor: bfloat16 [2, 2, 3584, 512], P('sect', 'tp', 'grp'), may hold values from -0.0625 to 0.0625
- adapter_output_factor: bfloat16 [2, 2, 3584, 256], P('sect', 'tp', 'grp'), may hold values from -1.5 to 1.5
- adapter_up_output: bfloat16 [2, 32, 16384], P('sect', None, 'grp'), may hold values from -1.5 to 1.5
- adapter_down_input: bfloat16 [2, 16, 16384], P('sect', None, 'grp'), may hold values from -0.1875 to 0.1875
Outputs:
- expert_out: bfloat16 [2, 512, 7168], P('sect', 'grp', 'tp')
- attention_out: bfloat16 [2, 512, 128, 512], P('sect', 'grp', 'tp')
Inputs may be any that keep to these rules, and one draw needn't show every extreme that they name: `row_expert_index`: each row names 8 different experts. Within the rows of one attention pair (aligned blocks of 8 rows) no expert is named more than 8 times, and in some blocks one expert is named exactly 8 times. `lengths`: in every aligned block of 8 sequences one sequence has exactly 512 cached rows.
All inputs are finite; a program needn't handle non-finite values.
Results may differ from a plain program's by a relative error of at most 0.008.
Values may be sent and summed in bfloat16 or wider, within the bound.
A program may use at most 128 MiB of HBM per device.

v0:
```python
import jax
import jax.numpy as jnp
from jax import lax
from jax.sharding import PartitionSpec as P

LAT = 512
QK = 192


def partner(value, axis, stride):
    mask = 2**stride
    pairs = [(source, source ^ mask) for source in range(lax.axis_size(axis))]
    return lax.ppermute(value, axis, pairs)


def attention_part(queries, latent_rotary_cache, lengths):
    query = queries[0]
    latent = latent_rotary_cache[0]
    scores = jnp.einsum("shk,slk->shl", query, latent, preferred_element_type=jnp.float32) * QK ** (
        -0.5
    )
    position = jnp.arange(latent.shape[1], dtype=jnp.int32)
    valid = position[None, None, :] < lengths[0][:, None, None]
    scores = jnp.where(valid, scores, -jnp.inf)
    top = jnp.max(scores, axis=2, keepdims=True)
    weights = jnp.exp(scores - top)
    probs = (weights / jnp.sum(weights, axis=2, keepdims=True)).astype(jnp.bfloat16)
    attended = jnp.einsum(
        "shl,slk->shk", probs, latent[:, :, :LAT], preferred_element_type=jnp.float32
    )
    return attended.astype(jnp.bfloat16)[None]


def adapter_factor_rows(factor, expert_table, quarter_parts):
    block_rows = factor.shape[0]
    width = factor.shape[1] // expert_table
    pieces = jnp.transpose(factor.reshape(block_rows, expert_table, width), (1, 0, 2))
    return jnp.repeat(pieces.reshape(expert_table, block_rows * width), quarter_parts, axis=0)


def body(
    queries,
    latent_rotary_cache,
    lengths,
    section_hidden_rows,
    row_expert_index,
    routing_gate_weight,
    gate_matrix,
    up_weight,
    down_weight,
    adapter_input_factor,
    adapter_output_factor,
    adapter_up_output,
    adapter_down_input,
):
    groups = lax.axis_size("grp")
    adapter_rank_size = adapter_down_input.shape[1]
    expert_table = adapter_input_factor.shape[3] // (2 * adapter_rank_size)
    quarter_parts = groups // expert_table
    capacity = section_hidden_rows.shape[1]
    half = section_hidden_rows.shape[2]
    ids = row_expert_index[0]
    gates = routing_gate_weight[0]
    labels = jnp.arange(expert_table, dtype=jnp.int32)
    match = ids[:, :, None] == labels[None, None, :]
    chosen = jnp.sum(match.astype(jnp.int32), axis=1)
    share = jnp.sum(jnp.where(match, gates[:, :, None], 0.0), axis=1)
    before = jnp.cumsum(chosen, axis=0) - chosen
    slot_ids = jnp.arange(capacity, dtype=jnp.int32)
    placed = (chosen.T[:, None, :] == 1) & (before.T[:, None, :] == slot_ids[None, :, None])
    placed_f = placed.astype(jnp.float32)
    slots = jnp.einsum(
        "ecr,rd->ecd",
        placed.astype(jnp.bfloat16),
        section_hidden_rows[0],
        preferred_element_type=jnp.float32,
    ).astype(jnp.bfloat16)
    outgoing_input = adapter_factor_rows(adapter_input_factor[0, 0], expert_table, quarter_parts)
    outgoing_output = adapter_factor_rows(adapter_output_factor[0, 0], expert_table, quarter_parts)
    send_rows = jnp.repeat(slots, quarter_parts, axis=0)
    received_rows, received_input, received_output = (
        lax.all_to_all(send_rows, "grp", split_axis=0, concat_axis=0, tiled=True),
        lax.all_to_all(outgoing_input, "grp", split_axis=0, concat_axis=0, tiled=True),
        lax.all_to_all(outgoing_output, "grp", split_axis=0, concat_axis=0, tiled=True),
    )
    received_rows, received_input, received_output, got_up, got_down = partner(
        (
            received_rows,
            received_input,
            received_output,
            adapter_up_output[0],
            adapter_down_input[0],
        ),
        "sect",
        0,
    )
    rows_in = received_rows.reshape(-1, half)
    factor_in = received_input.reshape(-1, 2 * adapter_rank_size)
    factor_out = received_output.reshape(-1, adapter_rank_size)
    gate_part = jnp.dot(rows_in, gate_matrix[0], preferred_element_type=jnp.float32)
    up_part = jnp.dot(rows_in, up_weight[0], preferred_element_type=jnp.float32)
    low_part = jnp.dot(rows_in, factor_in, preferred_element_type=jnp.float32)
    gate_sum, up_sum, low_sum = lax.psum((gate_part, up_part, low_part), "tp")
    low = low_sum.astype(jnp.bfloat16)
    gate = gate_sum + jnp.dot(
        low[:, :adapter_rank_size], got_up[:adapter_rank_size], preferred_element_type=jnp.float32
    )
    up = up_sum + jnp.dot(
        low[:, adapter_rank_size:], got_up[adapter_rank_size:], preferred_element_type=jnp.float32
    )
    hidden = (jax.nn.silu(gate) * up).astype(jnp.bfloat16)
    narrow = jnp.dot(hidden, got_down.T, preferred_element_type=jnp.float32)
    partial_value = jnp.dot(hidden, down_weight[0], preferred_element_type=jnp.float32) + jnp.dot(
        narrow, factor_out.T.astype(jnp.float32), precision=lax.Precision.HIGHEST
    )
    back = partial_value.reshape(groups, capacity, half)
    back = partner(back, "sect", 0)
    back = lax.all_to_all(back, "grp", split_axis=0, concat_axis=0, tiled=True)
    summed = jnp.sum(back.reshape(expert_table, quarter_parts, capacity, half), axis=1)
    weighted = placed_f * share.T[:, None, :]
    combined = jnp.einsum("ecr,ecd->rd", weighted, summed, precision=lax.Precision.HIGHEST)
    expert_out = combined.astype(jnp.bfloat16)[None]
    attention_out = attention_part(queries, latent_rotary_cache, lengths)
    return (expert_out, attention_out)


def solution(mesh):
    return jax.shard_map(
        body,
        mesh=mesh,
        in_specs=(
            P("sect", "grp", "tp", None),
            P("sect", "grp", None, None),
            P("sect", "grp"),
            P("sect", "grp", "tp"),
            P("sect", "grp", None),
            P("sect", "grp", None),
            P("sect", "tp", "grp"),
            P("sect", "tp", "grp"),
            P("sect", "grp", "tp"),
            P("sect", "tp", "grp", None),
            P("sect", "tp", "grp", None),
            P("sect", None, "grp"),
            P("sect", None, "grp"),
        ),
        out_specs=(P("sect", "grp", "tp"), P("sect", "grp", "tp", None)),
        check_vma=False,
    )
```

profile of v0, /device:TPU:8, one launch (start us, length us, event | category | flops | bytes accessed | tf_op | source)
XLA Modules:
  0.0 610.4 jit_solution(10745370875927088967)
XLA Ops:
  7.2 0.0 copy-start
  7.2 0.9 convert_reduce_fusion
  8.2 0.1 copy.43
  8.3 1.2 convolution_convert_fusion
  9.5 0.3 broadcast_in_dim.52
  9.7 0.0 copy-start.4
  9.7 0.0 copy-start.5
  9.8 97.7 %all_to_all.36 = bf16[64,8,3584]{2,1,0:T(8,128)(2,1)} all-to-all(bf16[64,8,3584]{2,1,0:T(8,128)(2,1)S(1)} %bitcast.77), channel_id=1, replica_groups=mesh['sect'=2,'grp'=64,'tp'=2] {'grp'}, dimensions={0} | all-to-all | bytes 7340032 | tf_op jit(solution)/shard_map/all_to_all | solution.py:82
  107.4 4.0 collective-permute-start
  111.5 0.1 copy.44
  111.6 0.2 copy.45
  111.8 0.2 reshape.70
  111.9 0.1 broadcast_in_dim.53
  112.0 0.1 all_to_all.30
  112.1 0.5 broadcast.30
  112.6 2.0 reduce
  114.7 0.7 reshape.78
  115.4 6.4 %all-to-all-start.1 = ((bf16[64,2,896]{2,1,0:T(2,128)(2,1)}), bf16[64,2,896]{2,1,0:T(2,128)(2,1)S(1)}, u32[]{:S(2)}, u32[]{:S(2)}) async-start(bf16[64,2,896]{2,1,0:T(2,128)(2,1)} %reshape.78), calls=%async_computation.1 | async-start | bytes 458752 | tf_op jit(solution)/shard_map/all_to_all | solution.py:83
  121.9 0.1 copy.47
  122.0 0.2 copy.48
  122.2 0.2 reshape.72
  122.4 0.1 all_to_all.31
  122.4 1.3 reduce.1
  123.8 0.8 reshape.80
  124.6 74.2 %all-to-all-done.1 = bf16[64,2,896]{2,1,0:T(2,128)(2,1)S(1)} async-done(((bf16[64,2,896]{2,1,0:T(2,128)(2,1)}), bf16[64,2,896]{2,1,0:T(2,128)(2,1)S(1)}, u32[]{:S(2)}, u32[]{:S(2)}) %all-to-all-start.1) | async-done | bytes 229408 | tf_op jit(solution)/shard_map/all_to_all | solution.py:83
  198.8 9.4 %all-to-all-start.2 = ((bf16[64,2,448]{2,1,0:T(2,128)(2,1)}), bf16[64,2,448]{2,1,0:T(2,128)(2,1)S(1)}, u32[]{:S(2)}, u32[]{:S(2)}) async-start(bf16[64,2,448]{2,1,0:T(2,128)(2,1)} %reshape.80), calls=%async_computation.2 | async-start | bytes 262144 | tf_op jit(solution)/shard_map/all_to_all | solution.py:84
  208.2 0.0 all-reduce.3.cloned.1.call-start
  208.3 0.2 reshape.79
  208.5 0.0 copy-start.9
  208.5 0.7 collective-permute-start.1
  209.2 4.5 fusion.11
  213.7 4.0 fusion.7
  217.7 0.0 all-reduce.3.cloned.1.call-update
  217.7 1.7 all-to-all-done.2
  219.4 0.2 reshape.81
  219.7 1.0 collective-permute-start.4
  220.7 1.1 collective-permute-start.2
  221.8 0.9 collective-permute-start.3
  222.7 1.8 collective-permute-done.4
  224.6 1.6 reshape.73
  226.2 0.6 reshape.71
  226.8 3.2 fusion.9
  230.0 3.6 psum.22
  233.7 0.3 fusion.37
  233.9 0.3 fusion.39
  234.2 15.2 %all-reduce.3.cloned.1.call-done = (f32[512,256]{1,0:T(8,128)}, f32[512,256]{1,0:T(8,128)}) async-done(((f32[512,256]{1,0:T(8,128)}, f32[512,256]{1,0:T(8,128)}), (f32[512,256]{1,0:T(8,128)}, f32[512,256]{1,0:T(8,128)})) %all-reduce.3.cloned.1.call-update) | async-done | bytes 1048592 | tf_op jit(solution)/shard_map/psum | solution.py:103
  249.4 1.4 multiply_convert_fusion
  250.8 1.1 fusion.13
  251.9 0.2 fusion.49
  252.1 3.5 add_bitcast_fusion
  255.6 1.6 collective-permute-start.5
  257.2 158.7 %collective-permute-done.5 = f32[64,8,3584]{2,1,0:T(8,128)} collective-permute-done((f32[64,8,3584]{2,1,0:T(8,128)S(1)}, f32[64,8,3584]{2,1,0:T(8,128)}, u32[]{:S(2)}, u32[]{:S(2)}) %collective-permute-start.5) | collective-permute-done | bytes 7340064 | tf_op jit(solution)/shard_map/ppermute | solution.py:13
  416.0 13.2 %all-to-all-start.3 = ((f32[64,8,3584]{2,1,0:T(8,128)}), f32[64,8,3584]{2,1,0:T(8,128)}, u32[]{:S(2)}, u32[]{:S(2)}) async-start(f32[64,8,3584]{2,1,0:T(8,128)} %collective-permute-done.5), calls=%async_computation.3 | async-start | bytes 14680064 | tf_op jit(solution)/shard_map/all_to_all | solution.py:118
  429.1 0.0 copy-start.7
  429.2 0.0 copy-start.8
  429.2 7.8 %copy.51 = bf16[1,8,512,576]{3,2,1,0:T(8,128)(2,1)} copy(bf16[1,8,512,576]{2,3,1,0:T(8,128)(2,1)} %param.14) | data formatting | bytes 9437184 | tf_op args[1]
  436.9 0.1 select_reduce_fusion
  437.1 0.1 iota_compare_fusion.2
  437.1 3.3 fusion.23
  440.4 0.3 fusion.48
  440.8 4.2 fusion.29
  445.0 151.2 %all-to-all-done.3 = f32[64,8,3584]{2,1,0:T(8,128)} async-done(((f32[64,8,3584]{2,1,0:T(8,128)}), f32[64,8,3584]{2,1,0:T(8,128)}, u32[]{:S(2)}, u32[]{:S(2)}) %all-to-all-start.3) | async-done | bytes 7340064 | tf_op jit(solution)/shard_map/all_to_all | solution.py:118
  596.2 4.0 bitcast_reduce_fusion
  600.1 3.4 fusion.4
  (29 shorter events, 0.2 us)
Async XLA Ops:
  7.2 243.6 %copy-start = (bf16[1,256,3584]{2,1,0:T(8,128)(2,1)S(1)}, bf16[1,256,3584]{2,1,0:T(8,128)(2,1)}, u32[]{:S(2)}) copy-start(bf16[1,256,3584]{2,1,0:T(8,128)(2,1)} %param.21) | copy-start | bytes 5505028
  9.7 101.8 %copy-start.4 = (bf16[1,1,56,512]{3,2,1,0:T(8,128)(2,1)S(1)}, bf16[1,1,56,512]{3,2,1,0:T(8,128)(2,1)}, u32[]{:S(2)}) copy-start(bf16[1,1,56,512]{3,2,1,0:T(8,128)(2,1)} %param.22) | copy-start | bytes 172036
  9.7 112.1 %copy-start.5 = (bf16[1,1,56,256]{3,2,1,0:T(8,128)(2,1)S(1)}, bf16[1,1,56,256]{3,2,1,0:T(8,128)(2,1)}, u32[]{:S(2)}) copy-start(bf16[1,1,56,256]{3,2,1,0:T(8,128)(2,1)} %param.23) | copy-start | bytes 86020
  107.4 101.8 %collective-permute-start = (bf16[64,8,3584]{2,1,0:T(8,128)(2,1)}, bf16[64,8,3584]{2,1,0:T(8,128)(2,1)}, u32[]{:S(2)}, u32[]{:S(2)}) collective-permute-start(bf16[64,8,3584]{2,1,0:T(8,128)(2,1)} %all_to_all.36), channel_id=1, source_target_pairs={{0,128},{128,0},{1,129},{129,1},{2,130},{130,2},{3,131},{131,3},{4... | collective-permute-start | bytes 11010056 | tf_op jit(solution)/shard_map/ppermute | solution.py:13
  115.4 83.4 %all-to-all-start.1 = ((bf16[64,2,896]{2,1,0:T(2,128)(2,1)}), bf16[64,2,896]{2,1,0:T(2,128)(2,1)S(1)}, u32[]{:S(2)}, u32[]{:S(2)}) async-start(bf16[64,2,896]{2,1,0:T(2,128)(2,1)} %reshape.78), calls=%async_computation.1 | async-start | bytes 458752 | tf_op jit(solution)/shard_map/all_to_all | solution.py:83
  198.8 20.6 %all-to-all-start.2 = ((bf16[64,2,448]{2,1,0:T(2,128)(2,1)}), bf16[64,2,448]{2,1,0:T(2,128)(2,1)S(1)}, u32[]{:S(2)}, u32[]{:S(2)}) async-start(bf16[64,2,448]{2,1,0:T(2,128)(2,1)} %reshape.80), calls=%async_computation.2 | async-start | bytes 262144 | tf_op jit(solution)/shard_map/all_to_all | solution.py:84
  208.2 41.2 %all-reduce.3.cloned.1.call-start = ((), (), s32[]{:S(2)}) async-start(), calls=%async_computation.4 | async-start | bytes 2097152 | tf_op jit(solution)/shard_map/psum | solution.py:103
  208.5 5.3 copy-start.9
  208.5 17.7 %collective-permute-start.1 = (bf16[64,1792]{1,0:T(8,128)(2,1)S(1)}, bf16[64,1792]{1,0:T(8,128)(2,1)S(1)}, u32[]{:S(2)}, u32[]{:S(2)}) collective-permute-start(bf16[64,1792]{1,0:T(8,128)(2,1)S(1)} %bitcast.81), channel_id=1, source_target_pairs={{0,128},{128,0},{1,129},{129,1},{2,130},{130,2},{3,131},{131,3},{4... | collective-permute-start | bytes 688136 | tf_op jit(solution)/shard_map/ppermute | solution.py:13
  213.7 7.0 %copy-start.10 = (bf16[1,32,256]{2,1,0:T(8,128)(2,1)S(1)}, bf16[1,32,256]{2,1,0:T(8,128)(2,1)}, u32[]{:S(2)}) copy-start(bf16[1,32,256]{2,1,0:T(8,128)(2,1)} %param.24) | copy-start | bytes 49156
  213.7 8.1 %copy-start.11 = (bf16[1,16,256]{2,1,0:T(8,128)(2,1)S(1)}, bf16[1,16,256]{2,1,0:T(8,128)(2,1)}, u32[]{:S(2)}) copy-start(bf16[1,16,256]{2,1,0:T(8,128)(2,1)} %param.25) | copy-start | bytes 24580
  219.7 4.9 collective-permute-start.4
  220.7 12.9 %collective-permute-start.2 = (bf16[32,256]{1,0:T(8,128)(2,1)S(1)}, bf16[32,256]{1,0:T(8,128)(2,1)S(1)}, u32[]{:S(2)}, u32[]{:S(2)}) collective-permute-start(bf16[32,256]{1,0:T(8,128)(2,1)S(1)} %bitcast.88), channel_id=1, source_target_pairs={{0,128},{128,0},{1,129},{129,1},{2,130},{130,2},{3,131},{131,3},{4... | collective-permute-start | bytes 49160 | tf_op jit(solution)/shard_map/ppermute | solution.py:13
  221.8 30.1 %collective-permute-start.3 = (bf16[16,256]{1,0:T(8,128)(2,1)S(1)}, bf16[16,256]{1,0:T(8,128)(2,1)S(1)}, u32[]{:S(2)}, u32[]{:S(2)}) collective-permute-start(bf16[16,256]{1,0:T(8,128)(2,1)S(1)} %bitcast.89), channel_id=1, source_target_pairs={{0,128},{128,0},{1,129},{129,1},{2,130},{130,2},{3,131},{131,3},{4... | collective-permute-start | bytes 24584 | tf_op jit(solution)/shard_map/ppermute | solution.py:13
  250.8 1.3 copy-start.2
  255.6 160.4 %collective-permute-start.5 = (f32[64,8,3584]{2,1,0:T(8,128)S(1)}, f32[64,8,3584]{2,1,0:T(8,128)}, u32[]{:S(2)}, u32[]{:S(2)}) collective-permute-start(f32[64,8,3584]{2,1,0:T(8,128)S(1)} %add_bitcast_fusion), channel_id=1, source_target_pairs={{0,128},{128,0},{1,129},{129,1},{2,130},{130,2},{3,131},{131,3},{4... | collective-permute-start | bytes 22020104 | tf_op jit(solution)/shard_map/ppermute | solution.py:13
  416.0 180.2 %all-to-all-start.3 = ((f32[64,8,3584]{2,1,0:T(8,128)}), f32[64,8,3584]{2,1,0:T(8,128)}, u32[]{:S(2)}, u32[]{:S(2)}) async-start(f32[64,8,3584]{2,1,0:T(8,128)} %collective-permute-done.5), calls=%async_computation.3 | async-start | bytes 14680064 | tf_op jit(solution)/shard_map/all_to_all | solution.py:118
  429.1 7.8 %copy-start.6 = (s32[1,8,8]{2,1,0:T(8,128)S(1)}, s32[1,8,8]{2,1,0:T(8,128)}, u32[]{:S(2)}) copy-start(s32[1,8,8]{2,1,0:T(8,128)} %param.17) | copy-start | bytes 772
  429.1 7.8 %copy-start.7 = (f32[1,8,8]{2,1,0:T(8,128)S(1)}, f32[1,8,8]{2,1,0:T(8,128)}, u32[]{:S(2)}) copy-start(f32[1,8,8]{2,1,0:T(8,128)} %param.18) | copy-start | bytes 772
  429.2 7.9 %copy-start.8 = (s32[1,8]{1,0:T(1,128)S(1)}, s32[1,8]{1,0:T(1,128)}, u32[]{:S(2)}) copy-start(s32[1,8]{1,0:T(1,128)} %param.15) | copy-start | bytes 100
  429.2 8.0 %copy-start.3 = (bf16[1,8,64,576]{3,2,1,0:T(8,128)(2,1)S(1)}, bf16[1,8,64,576]{3,2,1,0:T(8,128)(2,1)}, u32[]{:S(2)}) copy-start(bf16[1,8,64,576]{3,2,1,0:T(8,128)(2,1)} %param.13) | copy-start | bytes 1769476
  440.7 162.8 %copy-start.1 = (bf16[1,256,3584]{2,1,0:T(8,128)(2,1)S(1)}, bf16[1,256,3584]{2,1,0:T(8,128)(2,1)}, u32[]{:S(2)}) copy-start(bf16[1,256,3584]{2,1,0:T(8,128)(2,1)} %param.21) | copy-start | bytes 5505028
Sparse Core Ops, SparseCore 0:
  217.8 31.5 all-reduce.2
where the time goes:
time: 611 us; the launch traced here: 610 us
  waiting for transfers between devices  403 us (66%)
  blocking collectives  101 us (17%)
  starting transfers between devices  38.5 us (6%)
  matrix products  29.1 us (5%)
  between operations  14.4 us (2%)
  local copies, waits for them, and re-layouts  14.1 us (2%)
  other arithmetic  10.1 us (2%)
    ppermute x6, waiting for transfers between devices, partner(): return lax.ppermute(value, axis, pairs)  161 us
    all_to_all x1, waiting for transfers between devices, body(): back = lax.all_to_all(back, 'grp', split_axis=0, concat_axis=0, tiled=True)  151 us
    all_to_all x1, blocking collectives, body(): lax.all_to_all(send_rows, 'grp', split_axis=0, concat_axis=0, tiled=True)  97.7 us
    all_to_all x1, waiting for transfers between devices, body(): lax.all_to_all(outgoing_input, 'grp', split_axis=0, concat_axis=0, tiled=...  74.2 us
    psum x1, waiting for transfers between devices, body(): gate_sum, up_sum, low_sum = lax.psum((gate_part, up_part, low_part), 'tp')  15.2 us
    all_to_all x1, starting transfers between devices, body(): back = lax.all_to_all(back, 'grp', split_axis=0, concat_axis=0, tiled=True)  13.2 us
  transfers between devices with their start and end apart: 10, of which 6 were waited for; matrix products, arithmetic and copies ran while one was open for 6% of the time, Pallas kernels for 0%

commit v1 on v0

v1 whole, which is shorter than its diff:
```python
import jax
import jax.numpy as jnp
from jax import lax
from jax.experimental import pallas as pl
from jax.experimental.pallas import tpu as pltpu
from jax.sharding import PartitionSpec as P

LAT = 512
QK = 192
SEQ = 8
HEADS = 64
KD = 576
LEN = 512
HALF = 3584
QUARTER = HALF // 2
WIDE = HALF + 128
HID = 256
SLICE = 56
N_COPIES = 134
N_LOCAL = 17
BF = jnp.bfloat16
F32 = jnp.float32
MESH = pl.DeviceIdType.MESH

STEPS = (1, -1, 3, -3)
MIRROR = (1, 0, 3, 2)
CHAIN_SLOTS = ((0, 3), (1, 2))


def dot(a, b):
    return jnp.dot(a, b, preferred_element_type=F32)


def dot_nt(a, b):
    return lax.dot_general(a, b, (((1,), (1,)), ((), ())), preferred_element_type=F32)


def kernel(
    q_hbm,
    cache_hbm,
    len_hbm,
    rows_hbm,
    ids_hbm,
    gates_hbm,
    wg_hbm,
    wu_hbm,
    wd_hbm,
    ain_hbm,
    cout_hbm,
    bq_hbm,
    e_hbm,
    expert_hbm,
    att_hbm,
    unit,
    zbuf,
    x_ref,
    gu_own,
    gu_got,
    p_ref,
    ra,
    from_left,
    from_right,
    q_sum,
    ra2,
    from_left2,
    from_right2,
    z_send,
    z_got,
    out_buf,
    wg,
    wu,
    wd,
    ain,
    cout,
    bq_got,
    e_got,
    pieces,
    pieces_got,
    tx,
    t_ref,
    ct,
    bpad,
    epad,
    q_buf,
    cache,
    lens,
    ids,
    gates,
    att_buf,
    send_sem,
    recv_sem,
    local_sem,
):
    sect = lax.axis_index("sect")
    grp = lax.axis_index("grp")
    tp = lax.axis_index("tp")
    y = grp // 16
    zh = (grp // 4) % 4
    x = grp % 4
    z = zh * 2 + sect
    expert = grp // 4

    def plane(dy, dx):
        return (sect, ((y + dy) % 4) * 16 + zh * 4 + (x + dx) % 4, tp)

    def across(step, dy):
        target = (z + step + 8) % 8
        return (target % 2, ((y + dy) % 4) * 16 + (target // 2) * 4 + x, tp)

    other_core = (sect, grp, 1 - tp)
    partner = (1 - sect, grp, tp)
    count = [0]

    def remote(src, dst, device):
        i = count[0]
        count[0] += 1
        return pltpu.make_async_remote_copy(
            src_ref=src,
            dst_ref=dst,
            send_sem=send_sem.at[i],
            recv_sem=recv_sem.at[i],
            device_id=device,
            device_id_type=MESH,
        )

    local_count = [0]

    def local(src, dst):
        i = local_count[0]
        local_count[0] += 1
        copy = pltpu.make_async_copy(src, dst, local_sem.at[i])
        copy.start()
        return copy

    load_rows = local(rows_hbm.at[0], unit.at[:, pl.ds(0, HALF)])
    load_ids = local(ids_hbm.at[0], ids)
    load_gates = local(gates_hbm.at[0], gates)
    load_ain = local(ain_hbm.at[0, 0], ain)
    load_cout = local(cout_hbm.at[0, 0], cout)
    load_len = local(len_hbm, lens)
    load_q = local(q_hbm.at[0], q_buf)
    load_cache = local(cache_hbm.at[0], cache)
    load_wg = local(wg_hbm.at[0], wg)
    load_wu = local(wu_hbm.at[0], wu)
    load_wd = local(wd_hbm.at[0], wd)

    barrier = pltpu.get_barrier_semaphore()
    peers = [other_core, plane(1, 0), plane(-1 + 4, 0), plane(0, 1), plane(0, 3)]
    peers += [across(step, dy) for step in STEPS for dy in range(4)]
    for peer in peers:
        pl.semaphore_signal(barrier, inc=1, device_id=peer, device_id_type=MESH)

    load_ids.wait()
    load_gates.wait()
    lane8 = lax.broadcasted_iota(jnp.int32, (SEQ, 128), 1)
    named = lane8 % 32
    share = jnp.zeros((SEQ, 128), F32)
    for k in range(8):
        share += jnp.where(ids[:, k : k + 1] == named, gates[:, k : k + 1], 0.0)
    first = share.astype(BF).astype(F32)
    second = (share - first).astype(BF).astype(F32)
    third = share - first - second
    terms = jnp.where(lane8 < 32, first, jnp.where(lane8 < 64, second, third))
    load_rows.wait()
    unit[:, HALF:WIDE] = jnp.where(lane8 < 96, terms, 0.0).astype(BF)

    pl.semaphore_wait(barrier, len(peers))

    z_copies = [
        remote(unit, zbuf.at[MIRROR[slot]], across(STEPS[slot], 0)) for slot in range(4)
    ]
    for copy in z_copies:
        copy.start()
    bq_copy = remote(bq_hbm.at[0], bq_got, partner)
    e_copy = remote(e_hbm.at[0], e_got, partner)
    bq_copy.start()
    e_copy.start()

    load_ain.wait()
    load_cout.wait()
    lane56 = lax.broadcasted_iota(jnp.int32, (SLICE, 128), 1)
    shift = (y // 2) * 64
    mine = (lane56 >= shift) & (lane56 < shift + 64)
    place = lane56 % 64
    for e in range(16):
        a_tile = ain[:, 128 * (e // 4) : 128 * (e // 4) + 128].astype(F32)
        c_tile = cout[:, 128 * (e // 8) : 128 * (e // 8) + 128].astype(F32)
        a_at, c_at = 32 * (e % 4), 16 * (e % 8)

        def turned(tile, by):
            by = by % 128
            return tile if by == 0 else pltpu.roll(tile, by, 1)

        low = jnp.where(
            place < 32,
            turned(a_tile, -a_at),
            jnp.where(place < 48, turned(c_tile, 32 - c_at), turned(c_tile, 48 - c_at)),
        )
        low = jnp.where(lane56 < 64, low, 0.0)
        both = low + pltpu.roll(low, 64, 1)
        pieces[e] = jnp.where(mine, both, 0.0).astype(BF)
    piece_copies = []
    for step in STEPS:
        for dy in range(4):
            target = (z + step + 8) % 8
            aim = ((y + dy) % 4) * 4 + target // 2
            copy = remote(pieces.at[aim], pieces_got.at[y * 4 + zh], across(step, dy))
            copy.start()
            piece_copies.append(copy)

    def attend(first_seq, n):
        def one(s, carry):
            cached = cache[s]
            query = q_buf[s]
            scores = dot(query[:, :LAT], cached[:LAT]) + dot(query[:, LAT:], cached[LAT:])
            scores = scores * QK ** (-0.5)
            position = lax.broadcasted_iota(jnp.int32, (HEADS, LEN), 1)
            at = lax.broadcasted_iota(jnp.int32, (1, SEQ), 1) == s
            limit = jnp.sum(jnp.where(at, lens[...], 0), axis=1, keepdims=True)
            scores = jnp.where(position < limit, scores, -jnp.inf)
            top = jnp.max(scores, axis=1, keepdims=True)
            weights = jnp.exp(scores - top)
            probs = (weights / jnp.sum(weights, axis=1, keepdims=True)).astype(BF)
            att_buf[s] = dot_nt(probs, cached[:LAT]).astype(BF)
            return carry

        lax.fori_loop(first_seq, first_seq + n, one, 0)

    def rows_of(chain, du):
        return pl.ds((chain * 4 + du) * 16, 16)

    along = [
        dict(up=plane(0, 1), um=plane(0, 3), vp=plane(1, 0), vm=plane(3, 0)),
        dict(up=plane(1, 0), um=plane(3, 0), vp=plane(0, 1), vm=plane(0, 3)),
    ]
    left_x, right_x = pl.ds(0, QUARTER), pl.ds(QUARTER, WIDE - QUARTER)
    left, right = pl.ds(0, QUARTER), pl.ds(QUARTER, QUARTER)

    u_p, u_m, u_fp, u_fm = [], [], [], []
    v_p, v_m, v_fp, v_fm = [], [], [], []
    for c in range(2):
        d = along[c]
        own = x_ref.at[0, rows_of(c, 0)]
        u_p.append(remote(own, x_ref.at[0, rows_of(c, 3)], d["up"]))
        u_m.append(remote(own, x_ref.at[0, rows_of(c, 1)], d["um"]))
        u_fp.append(
            remote(
                x_ref.at[0, rows_of(c, 3), left_x], x_ref.at[0, rows_of(c, 2), left_x], d["up"]
            )
        )
        u_fm.append(
            remote(
                x_ref.at[0, rows_of(c, 1), right_x], x_ref.at[0, rows_of(c, 2), right_x], d["um"]
            )
        )
        v_p.append([])
        v_m.append([])
        v_fp.append([])
        v_fm.append([])
        for du in range(4):
            r = rows_of(c, du)
            v_p[c].append(remote(x_ref.at[0, r], x_ref.at[3, r], d["vp"]))
            v_m[c].append(remote(x_ref.at[0, r], x_ref.at[1, r], d["vm"]))
            v_fp[c].append(
                remote(x_ref.at[3, r, left_x], x_ref.at[2, r, left_x], d["vp"])
            )
            v_fm[c].append(
                remote(x_ref.at[1, r, right_x], x_ref.at[2, r, right_x], d["vm"])
            )

    for c in range(2):
        for slot in CHAIN_SLOTS[c]:
            z_copies[MIRROR[slot]].wait_recv()
        a, b = CHAIN_SLOTS[c]
        x_ref[0, rows_of(c, 0)] = jnp.concatenate([zbuf[a], zbuf[b]], axis=0)
        u_p[c].start()
        u_m[c].start()
        v_p[c][0].start()
        v_m[c][0].start()

    load_len.wait()
    load_q.wait()
    load_cache.wait()
    attend(0, 2)

    def spread(c, du):
        v_p[c][du].start()
        v_m[c][du].start()

    def forward(c, du):
        v_p[c][du].wait_recv()
        v_fp[c][du].start()
        v_m[c][du].wait_recv()
        v_fm[c][du].start()

    for c in range(2):
        u_p[c].wait_recv()
        u_fp[c].start()
        u_m[c].wait_recv()
        u_fm[c].start()
        spread(c, 3)
        spread(c, 1)

    for copy in piece_copies:
        copy.wait_recv()
    for k in range(8):
        joined = pieces_got[k].astype(F32) + pieces_got[k + 8].astype(F32)
        tx[x, k] = joined.astype(BF)
    before, after = (x + 3) % 4, (x + 1) % 4
    t_p = remote(tx.at[x], tx.at[x], plane(0, 1))
    t_m = remote(tx.at[x], tx.at[x], plane(0, 3))
    t_fp = remote(tx.at[before, pl.ds(0, 4)], tx.at[before, pl.ds(0, 4)], plane(0, 1))
    t_fm = remote(tx.at[after, pl.ds(4, 4)], tx.at[after, pl.ds(4, 4)], plane(0, 3))
    t_p.start()
    t_m.start()

    for c in range(2):
        forward(c, 0)
    for c in range(2):
        u_fp[c].wait_recv()
        u_fm[c].wait_recv()
        spread(c, 2)

    t_p.wait_recv()
    t_fp.start()
    t_m.wait_recv()
    t_fm.start()

    attend(2, 2)

    for c in range(2):
        forward(c, 3)
        forward(c, 1)

    t_fp.wait_recv()
    t_fm.wait_recv()
    for k in range(8):
        block = jnp.concatenate([tx[i, k].astype(F32) for i in range(4)], axis=0)
        t_ref[224 * k : 224 * k + 224] = block.astype(BF)
    for k in range(14):
        block = t_ref[128 * k : 128 * k + 128].astype(F32)
        ct[:, 128 * k : 128 * k + 128] = block.T.astype(BF)
    bq_copy.wait_recv()
    e_copy.wait_recv()
    bpad[...] = jnp.zeros_like(bpad)
    bpad[0:16, 0:HID] = bq_got[0:16]
    bpad[16:32, HID : 2 * HID] = bq_got[16:32]
    epad[...] = jnp.zeros_like(epad)
    for at in (32, 48, 96, 112):
        epad[at : at + 16] = e_got[...]

    load_wg.wait()
    load_wu.wait()
    load_wd.wait()

    lane128 = lax.broadcasted_iota(jnp.int32, (128, 128), 1)
    exchange = [
        remote(gu_own.at[dv], gu_got.at[dv], other_core) for dv in range(4)
    ]

    def first_product(dv):
        gu_own[dv, :, 0:HID] = dot(x_ref[dv, :, 0:HALF], wg[...])
        gu_own[dv, :, HID : 2 * HID] = dot(x_ref[dv, :, 0:HALF], wu[...])
        low_a = dot(x_ref[dv, :, 0:QUARTER], t_ref[...])
        low_b = dot(x_ref[dv, :, QUARTER:HALF], t_ref[...])
        gu_own[dv, :, 2 * HID :] = low_a + pltpu.roll(low_b, 64, 1)
        exchange[dv].start()

    def second_product(dv):
        exchange[dv].wait_recv()
        low = (gu_own[dv, :, 2 * HID :] + gu_got[dv, :, 2 * HID :]).astype(BF)
        extra = dot(low, bpad[...])
        gate = gu_own[dv, :, 0:HID] + gu_got[dv, :, 0:HID] + extra[:, 0:HID]
        up = gu_own[dv, :, HID : 2 * HID] + gu_got[dv, :, HID : 2 * HID] + extra[:, HID:]
        hidden = (gate / (1.0 + jnp.exp(-gate)) * up).astype(BF)
        narrow = dot_nt(hidden, epad[...])
        head = narrow.astype(BF).astype(F32)
        rest = narrow - head
        split = jnp.where((lane128 % 64) < 48, head, rest)
        picks = (lane128 % 32 == expert) & (lane128 < 96)
        shares = x_ref[dv, :, HALF:WIDE].astype(F32)
        share = jnp.sum(jnp.where(picks, shares, 0.0), axis=1, keepdims=True)
        for h in range(2):
            keep = (lane128 // 64) == h
            thin = jnp.where(keep, split, 0.0).astype(BF)

            def tile(i, carry):
                at = pl.multiple_of(i * HID, HID)
                there = pl.multiple_of(h * QUARTER + i * HID, HID)
                value = dot(hidden, wd[:, pl.ds(there, HID)]) + dot(thin, ct[:, pl.ds(at, HID)])
                p_ref[dv, :, pl.ds(there, HID)] = (value * share).astype(BF)
                return carry

            lax.fori_loop(0, QUARTER // HID, tile, 0)

    first_product(0)
    for c in range(2):
        forward(c, 2)
    first_product(1)
    first_product(3)
    second_product(0)

    a_p, a_m, b_p, b_m, c_p, c_m = [], [], [], [], [], []
    for c in range(2):
        d = along[c]
        for group in (a_p, a_m, b_p, b_m, c_p, c_m):
            group.append([])
        for du in range(4):
            r = rows_of(c, du)
            a_p[c].append(remote(p_ref.at[2, r, left], ra.at[0, r], d["vp"]))
            a_m[c].append(remote(p_ref.at[2, r, right], ra.at[1, r], d["vm"]))
            b_p[c].append(remote(p_ref.at[1, r, right], from_left.at[r, right], d["vp"]))
            b_m[c].append(remote(p_ref.at[3, r, left], from_right.at[r, left], d["vm"]))
            c_p[c].append(remote(p_ref.at[1, r, left], from_left.at[r, left], d["vp"]))
            c_m[c].append(remote(p_ref.at[3, r, right], from_right.at[r, right], d["vm"]))
    order = (2, 1, 3, 0)

    second_product(1)
    for c in range(2):
        for du in order:
            b_p[c][du].start()
    second_product(3)
    for c in range(2):
        for du in order:
            b_m[c][du].start()
    for c in range(2):
        for du in range(4):
            v_fp[c][du].wait_recv()
            v_fm[c][du].wait_recv()
    first_product(2)
    attend(4, 1)
    second_product(2)
    for du in order:
        for c in range(2):
            a_p[c][du].start()
            a_m[c][du].start()
    attend(5, 3)
    store_att = local(att_buf, att_hbm.at[0])

    for copy in z_copies + [bq_copy, e_copy] + piece_copies + [t_p, t_m, t_fp, t_fm]:
        copy.wait_send()
    for c in range(2):
        for copy in [u_p[c], u_m[c], u_fp[c], u_fm[c]] + v_p[c] + v_m[c] + v_fp[c] + v_fm[c]:
            copy.wait_send()
    for copy in exchange:
        copy.wait_send()

    for du in order:
        for c in range(2):
            r = rows_of(c, du)
            a_p[c][du].wait_recv()
            p_ref[1, r, left] = (p_ref[1, r, left].astype(F32) + ra[0, r].astype(F32)).astype(BF)
            c_p[c][du].start()
            a_m[c][du].wait_recv()
            p_ref[3, r, right] = (p_ref[3, r, right].astype(F32) + ra[1, r].astype(F32)).astype(BF)
            c_m[c][du].start()

    def gather_v(c, du):
        r = rows_of(c, du)
        for copy in (b_p[c][du], c_p[c][du], b_m[c][du], c_m[c][du]):
            copy.wait_recv()
        total = p_ref[0, r].astype(F32) + from_left[r].astype(F32) + from_right[r].astype(F32)
        q_sum[r] = total.astype(BF)

    a2p, a2m, b2p, b2m, c2p, c2m = [], [], [], [], [], []
    for c in range(2):
        d = along[c]
        r1, r2, r3 = rows_of(c, 1), rows_of(c, 2), rows_of(c, 3)
        a2p.append(remote(q_sum.at[r2, left], ra2.at[0, c], d["up"]))
        a2m.append(remote(q_sum.at[r2, right], ra2.at[1, c], d["um"]))
        b2p.append(remote(q_sum.at[r1, right], from_left2.at[c, :, right], d["up"]))
        b2m.append(remote(q_sum.at[r3, left], from_right2.at[c, :, left], d["um"]))
        c2p.append(remote(q_sum.at[r1, left], from_left2.at[c, :, left], d["up"]))
        c2m.append(remote(q_sum.at[r3, right], from_right2.at[c, :, right], d["um"]))
    for c in range(2):
        gather_v(c, 2)
        a2p[c].start()
        a2m[c].start()
    for c in range(2):
        gather_v(c, 1)
        b2p[c].start()
    for c in range(2):
        gather_v(c, 3)
        b2m[c].start()
    for c in range(2):
        r1, r3 = rows_of(c, 1), rows_of(c, 3)
        a2p[c].wait_recv()
        q_sum[r1, left] = (q_sum[r1, left].astype(F32) + ra2[0, c].astype(F32)).astype(BF)
        c2p[c].start()
        a2m[c].wait_recv()
        q_sum[r3, right] = (q_sum[r3, right].astype(F32) + ra2[1, c].astype(F32)).astype(BF)
        c2m[c].start()
    for c in range(2):
        gather_v(c, 0)

    z_back = [remote(z_send.at[slot], z_got.at[MIRROR[slot]], across(STEPS[slot], 0)) for slot in range(4)]
    for c in range(2):
        for copy in (b2p[c], c2p[c], b2m[c], c2m[c]):
            copy.wait_recv()
        total = (
            q_sum[rows_of(c, 0)].astype(F32)
            + from_left2[c].astype(F32)
            + from_right2[c].astype(F32)
        )
        for i in range(2):
            slot = CHAIN_SLOTS[c][i]
            z_send[slot] = total[8 * i : 8 * i + 8].astype(BF)
            z_back[slot].start()

    for c in range(2):
        for group in (a_p, a_m, b_p, b_m, c_p, c_m):
            for copy in group[c]:
                copy.wait_send()
        for copy in (a2p[c], a2m[c], b2p[c], b2m[c], c2p[c], c2m[c]):
            copy.wait_send()
    store_att.wait()
    for copy in z_back:
        copy.wait_recv()
    result = z_got[0].astype(F32) + z_got[1].astype(F32) + z_got[2].astype(F32) + z_got[3].astype(F32)
    out_buf[...] = result.astype(BF)
    store_out = local(out_buf, expert_hbm.at[0])
    for copy in z_back:
        copy.wait_send()
    store_out.wait()
    assert count[0] == N_COPIES, count[0]


def body(
    queries,
    latent_rotary_cache,
    lengths,
    section_hidden_rows,
    row_expert_index,
    routing_gate_weight,
    gate_matrix,
    up_weight,
    down_weight,
    adapter_input_factor,
    adapter_output_factor,
    adapter_up_output,
    adapter_down_input,
):
    vmem = pltpu.VMEM
    expert_out, attention_out = pl.pallas_call(
        kernel,
        out_shape=(
            jax.ShapeDtypeStruct((1, SEQ, HALF), BF),
            jax.ShapeDtypeStruct((1, SEQ, HEADS, LAT), BF),
        ),
        in_specs=[pl.BlockSpec(memory_space=pl.ANY)] * 13,
        out_specs=[pl.BlockSpec(memory_space=pl.ANY)] * 2,
        scratch_shapes=[
            vmem((SEQ, WIDE), BF),
            vmem((4, SEQ, WIDE), BF),
            vmem((4, 128, WIDE), BF),
            vmem((4, 128, 2 * HID + 128), F32),
            vmem((4, 128, 2 * HID + 128), F32),
            vmem((4, 128, HALF), BF),
            vmem((2, 128, QUARTER), BF),
            vmem((128, HALF), BF),
            vmem((128, HALF), BF),
            vmem((128, HALF), BF),
            vmem((2, 2, 16, QUARTER), BF),
            vmem((2, 16, HALF), BF),
            vmem((2, 16, HALF), BF),
            vmem((4, SEQ, HALF), BF),
            vmem((4, SEQ, HALF), BF),
            vmem((SEQ, HALF), BF),
            vmem((HALF, HID), BF),
            vmem((HALF, HID), BF),
            vmem((HID, HALF), BF),
            vmem((SLICE, 512), BF),
            vmem((SLICE, 256), BF),
            vmem((32, HID), BF),
            vmem((16, HID), BF),
            vmem((16, SLICE, 128), BF),
            vmem((16, SLICE, 128), BF),
            vmem((4, 8, SLICE, 128), BF),
            vmem((QUARTER, 128), BF),
            vmem((128, QUARTER), BF),
            vmem((128, 2 * HID), BF),
            vmem((128, HID), BF),
            vmem((SEQ, HEADS, KD), BF),
            vmem((SEQ, KD, LEN), BF),
            vmem((1, SEQ), jnp.int32),
            vmem((SEQ, 8), jnp.int32),
            vmem((SEQ, 8), F32),
            vmem((SEQ, HEADS, LAT), BF),
            pltpu.SemaphoreType.DMA((N_COPIES,)),
            pltpu.SemaphoreType.DMA((N_COPIES,)),
            pltpu.SemaphoreType.DMA((N_LOCAL,)),
        ],
        compiler_params=pltpu.CompilerParams(
            collective_id=0, has_side_effects=True, vmem_limit_bytes=56 * 1024 * 1024
        ),
    )(
        queries,
        jnp.swapaxes(latent_rotary_cache, 2, 3),
        lengths,
        section_hidden_rows,
        row_expert_index,
        routing_gate_weight,
        gate_matrix,
        up_weight,
        down_weight,
        adapter_input_factor,
        adapter_output_factor,
        adapter_up_output,
        adapter_down_input,
    )
    return (expert_out, attention_out)


def solution(mesh):
    return jax.shard_map(
        body,
        mesh=mesh,
        in_specs=(
            P("sect", "grp", "tp", None),
            P("sect", "grp", None, None),
            P("sect", "grp"),
            P("sect", "grp", "tp"),
            P("sect", "grp", None),
            P("sect", "grp", None),
            P("sect", "tp", "grp"),
            P("sect", "tp", "grp"),
            P("sect", "grp", "tp"),
            P("sect", "tp", "grp", None),
            P("sect", "tp", "grp", None),
            P("sect", None, "grp"),
            P("sect", None, "grp"),
        ),
        out_specs=(P("sect", "grp", "tp"), P("sect", "grp", "tp", None)),
        check_vma=False,
    )
```

time: 611 us -> 91.2 us (0.15)
  waiting for transfers between devices: 403 us -> 0 us
  blocking collectives: 101 us -> 0 us
  Pallas kernels: 0 us -> 85.5 us
  starting transfers between devices: 38.5 us -> 0 us
  matrix products: 29.1 us -> 0 us
  between operations: 14.4 us -> 0.64 us
  local copies, waits for them, and re-layouts: 14.1 us -> 3.31 us
  other arithmetic: 10.1 us -> 0 us
    all_to_all x3 -> x0, waiting for transfers between devices: 227 us -> none  [the longest x1 151 us: body(): back = lax.all_to_all(back, 'grp', split_axis=0, concat_axis=0, tiled=True)]
    ppermute x6 -> x0, waiting for transfers between devices: 161 us -> none  [partner(): return lax.ppermute(value, axis, pairs)]
    all_to_all x1 -> x0, blocking collectives: 97.7 us -> none  [body(): lax.all_to_all(send_rows, 'grp', split_axis=0, concat_axis=0, tiled=True)]
    pallas_call x0 -> x1, Pallas kernels: none -> 85.5 us  [body(): pl.pallas_call(kernel, out_shape=(jax.ShapeDtypeStruct((1, SEQ, HALF), BF...]
    dot_general x12 -> x0, matrix products: 29.1 us -> none  [the longest x1 4.52 us: body(): jnp.dot(rows_in, gate_matrix[0], preferred_element_type=jnp.float32)]
    all_to_all x3 -> x0, starting transfers between devices: 29 us -> none  [the longest x1 13.2 us: body(): back = lax.all_to_all(back, 'grp', split_axis=0, concat_axis=0, tiled=True)]
    psum x1 -> x0, waiting for transfers between devices: 15.2 us -> none  [body(): gate_sum, up_sum, low_sum = lax.psum((gate_part, up_part, low_part), 'tp')]
    ppermute x6 -> x0, starting transfers between devices: 9.43 us -> none  [partner(): return lax.ppermute(value, axis, pairs)]
  transfers between devices with their start and end apart: 10 -> 0, of which waited for: 6 -> 0; matrix products, arithmetic and copies ran while one was open for 6% -> 0% of each run, Pallas kernels for 0% -> 0%
where the time goes in v1:
time: 91.2 us; the launch traced here: 89.5 us
  Pallas kernels  85.5 us (94%)
  local copies, waits for them, and re-layouts  3.31 us (4%)
    pallas_call x1, Pallas kernels, body(): pl.pallas_call(kernel, out_shape=(jax.ShapeDtypeStruct((1, SEQ, HALF), BF...  85.5 us
    unnamed x2, local copies, waits for them, and re-layouts  3.31 us

profile of v1, /device:TPU:8, one launch (start us, length us, event | category | flops | bytes accessed | tf_op | source)
XLA Modules:
  0.0 89.5 jit_solution(14925411864526823011)
XLA Ops:
  0.6 85.5 %shard_map.140 = (bf16[1,8,3584]{2,1,0:T(8,128)(2,1)}, bf16[1,8,64,512]{3,2,1,0:T(8,128)(2,1)}) custom-call(bf16[1,8,64,576]{3,2,1,0:T(8,128)(2,1)} %q_hbm.1, bf16[1,8,576,512]{3,2,1,0:T(8,128)(2,1)} %bitcast.1, s32[1,8]{1,0:T(1,128)} %len_hbm.1, bf16[1,8,3584]{2,1,0:T(8,128)(2,1)} %rows_hbm.1, s32[1,8,8]{2,1,0:T(8,128)} %ids_hbm.1, f32[1,8,8]{2,1,0:T(8,128)} %gates_hbm.1, ...), custom_call_target="tpu_custom_call" | custom-call | tf_op jit(solution)/shard_map/pallas_call | solution.py:544
  86.2 1.4 %copy.17 = bf16[1,8,3584]{2,1,0:T(8,128)(2,1)} copy(bf16[1,8,3584]{2,1,0:T(8,128)(2,1)} %get-tuple-element.4) | data formatting | bytes 114688
  87.6 1.9 %copy.18 = bf16[1,8,64,512]{3,2,1,0:T(8,128)(2,1)} copy(bf16[1,8,64,512]{3,2,1,0:T(8,128)(2,1)} %get-tuple-element.5) | data formatting | bytes 1048576

commit v2 on v1

--- a/solution.py
+++ b/solution.py
@@ -16,15 +16,15 @@
 WIDE = HALF + 128
 HID = 256
 SLICE = 56
-N_COPIES = 134
-N_LOCAL = 17
+N_COPIES = 133
+N_LOCAL = 16
 BF = jnp.bfloat16
 F32 = jnp.float32
 MESH = pl.DeviceIdType.MESH
 
 STEPS = (1, -1, 3, -3)
 MIRROR = (1, 0, 3, 2)
-CHAIN_SLOTS = ((0, 3), (1, 2))
+CHAIN_SLOTS = ((0, 1), (2, 3))
 
 
 def dot(a, b):
@@ -49,7 +49,7 @@
     cout_hbm,
     bq_hbm,
     e_hbm,
-    expert_hbm,
+    z_got,
     att_hbm,
     unit,
     zbuf,
@@ -65,8 +65,6 @@
     from_left2,
     from_right2,
     z_send,
-    z_got,
-    out_buf,
     wg,
     wu,
     wd,
@@ -76,6 +74,7 @@
     e_got,
     pieces,
     pieces_got,
+    joined,
     tx,
     t_ref,
     ct,
@@ -103,9 +102,9 @@
     def plane(dy, dx):
         return (sect, ((y + dy) % 4) * 16 + zh * 4 + (x + dx) % 4, tp)
 
-    def across(step, dy):
+    def across(step):
         target = (z + step + 8) % 8
-        return (target % 2, ((y + dy) % 4) * 16 + (target // 2) * 4 + x, tp)
+        return (target % 2, y * 16 + (target // 2) * 4 + x, tp)
 
     other_core = (sect, grp, 1 - tp)
     partner = (1 - sect, grp, tp)
@@ -132,6 +131,12 @@
         copy.start()
         return copy
 
+    barrier = pltpu.get_barrier_semaphore()
+    peers = [other_core, plane(1, 0), plane(2, 0), plane(3, 0), plane(0, 1), plane(0, 3)]
+    peers += [across(step) for step in STEPS]
+    for peer in peers:
+        pl.semaphore_signal(barrier, inc=1, device_id=peer, device_id_type=MESH)
+
     load_rows = local(rows_hbm.at[0], unit.at[:, pl.ds(0, HALF)])
     load_ids = local(ids_hbm.at[0], ids)
     load_gates = local(gates_hbm.at[0], gates)
@@ -143,12 +148,6 @@
     load_wg = local(wg_hbm.at[0], wg)
     load_wu = local(wu_hbm.at[0], wu)
     load_wd = local(wd_hbm.at[0], wd)
-
-    barrier = pltpu.get_barrier_semaphore()
-    peers = [other_core, plane(1, 0), plane(-1 + 4, 0), plane(0, 1), plane(0, 3)]
-    peers += [across(step, dy) for step in STEPS for dy in range(4)]
-    for peer in peers:
-        pl.semaphore_signal(barrier, inc=1, device_id=peer, device_id_type=MESH)
 
     load_ids.wait()
     load_gates.wait()
@@ -167,7 +166,7 @@
     pl.semaphore_wait(barrier, len(peers))
 
     z_copies = [
-        remote(unit, zbuf.at[MIRROR[slot]], across(STEPS[slot], 0)) for slot in range(4)
+        remote(unit, zbuf.at[MIRROR[slot]], across(STEPS[slot])) for slot in range(4)
     ]
     for copy in z_copies:
         copy.start()
@@ -199,14 +198,15 @@
         low = jnp.where(lane56 < 64, low, 0.0)
         both = low + pltpu.roll(low, 64, 1)
         pieces[e] = jnp.where(mine, both, 0.0).astype(BF)
-    piece_copies = []
-    for step in STEPS:
-        for dy in range(4):
-            target = (z + step + 8) % 8
-            aim = ((y + dy) % 4) * 4 + target // 2
-            copy = remote(pieces.at[aim], pieces_got.at[y * 4 + zh], across(step, dy))
-            copy.start()
-            piece_copies.append(copy)
+    y_copies = [
+        remote(
+            pieces.at[pl.ds(((y + dy) % 4) * 4, 4)], pieces_got.at[y], plane(dy, 0)
+        )
+        for dy in (1, 3, 2)
+    ]
+    for copy in y_copies:
+        copy.start()
+    pieces_got[y] = pieces[pl.ds(y * 4, 4)]
 
     def attend(first_seq, n):
         def one(s, carry):
@@ -268,7 +268,7 @@
                 remote(x_ref.at[1, r, right_x], x_ref.at[2, r, right_x], d["vm"])
             )
 
-    for c in range(2):
+    def enter(c):
         for slot in CHAIN_SLOTS[c]:
             z_copies[MIRROR[slot]].wait_recv()
         a, b = CHAIN_SLOTS[c]
@@ -278,11 +278,6 @@
         v_p[c][0].start()
         v_m[c][0].start()
 
-    load_len.wait()
-    load_q.wait()
-    load_cache.wait()
-    attend(0, 2)
-
     def spread(c, du):
         v_p[c][du].start()
         v_m[c][du].start()
@@ -293,7 +288,7 @@
         v_m[c][du].wait_recv()
         v_fm[c][du].start()
 
-    for c in range(2):
+    def turn(c):
         u_p[c].wait_recv()
         u_fp[c].start()
         u_m[c].wait_recv()
@@ -301,45 +296,49 @@
         spread(c, 3)
         spread(c, 1)
 
-    for copy in piece_copies:
+    def turn_far(c):
+        u_fp[c].wait_recv()
+        u_fm[c].wait_recv()
+        spread(c, 2)
+
+    enter(0)
+
+    for copy in y_copies:
         copy.wait_recv()
-    for k in range(8):
-        joined = pieces_got[k].astype(F32) + pieces_got[k + 8].astype(F32)
-        tx[x, k] = joined.astype(BF)
+    for k in range(4):
+        for i in range(2):
+            both = pieces_got[i, k].astype(F32) + pieces_got[i + 2, k].astype(F32)
+            joined[k, i] = both.astype(BF)
+    t_copies = [
+        remote(joined.at[((z + step + 8) % 8) // 2], tx.at[x, zh], across(step)) for step in STEPS
+    ]
+    for copy in t_copies:
+        copy.start()
+
+    enter(1)
+    load_len.wait()
+    load_q.wait()
+    load_cache.wait()
+    attend(0, 1)
+    turn(0)
+    attend(1, 1)
+    turn(1)
+
+    for copy in t_copies:
+        copy.wait_recv()
     before, after = (x + 3) % 4, (x + 1) % 4
     t_p = remote(tx.at[x], tx.at[x], plane(0, 1))
     t_m = remote(tx.at[x], tx.at[x], plane(0, 3))
-    t_fp = remote(tx.at[before, pl.ds(0, 4)], tx.at[before, pl.ds(0, 4)], plane(0, 1))
-    t_fm = remote(tx.at[after, pl.ds(4, 4)], tx.at[after, pl.ds(4, 4)], plane(0, 3))
+    t_fp = remote(tx.at[before, pl.ds(0, 2)], tx.at[before, pl.ds(0, 2)], plane(0, 1))
+    t_fm = remote(tx.at[after, pl.ds(2, 2)], tx.at[after, pl.ds(2, 2)], plane(0, 3))
     t_p.start()
     t_m.start()
 
-    for c in range(2):
-        forward(c, 0)
-    for c in range(2):
-        u_fp[c].wait_recv()
-        u_fm[c].wait_recv()
-        spread(c, 2)
-
-    t_p.wait_recv()
-    t_fp.start()
-    t_m.wait_recv()
-    t_fm.start()
-
-    attend(2, 2)
-
-    for c in range(2):
-        forward(c, 3)
-        forward(c, 1)
-
-    t_fp.wait_recv()
-    t_fm.wait_recv()
-    for k in range(8):
-        block = jnp.concatenate([tx[i, k].astype(F32) for i in range(4)], axis=0)
-        t_ref[224 * k : 224 * k + 224] = block.astype(BF)
-    for k in range(14):
-        block = t_ref[128 * k : 128 * k + 128].astype(F32)
-        ct[:, 128 * k : 128 * k + 128] = block.T.astype(BF)
+    forward(0, 0)
+    turn_far(0)
+    forward(1, 0)
+    turn_far(1)
+
     bq_copy.wait_recv()
     e_copy.wait_recv()
     bpad[...] = jnp.zeros_like(bpad)
@@ -349,30 +348,42 @@
     for at in (32, 48, 96, 112):
         epad[at : at + 16] = e_got[...]
 
-    load_wg.wait()
-    load_wu.wait()
-    load_wd.wait()
-
     lane128 = lax.broadcasted_iota(jnp.int32, (128, 128), 1)
+    low_at, gate_at, up_at = (
+        pl.ds(2 * HID, 128),
+        pl.ds(0, HID),
+        pl.ds(HID, HID),
+    )
     exchange = [
-        remote(gu_own.at[dv], gu_got.at[dv], other_core) for dv in range(4)
+        [
+            remote(gu_own.at[dv, :, at], gu_got.at[dv, :, at], other_core)
+            for at in (gate_at, up_at, low_at)
+        ]
+        for dv in range(4)
     ]
 
-    def first_product(dv):
-        gu_own[dv, :, 0:HID] = dot(x_ref[dv, :, 0:HALF], wg[...])
-        gu_own[dv, :, HID : 2 * HID] = dot(x_ref[dv, :, 0:HALF], wu[...])
+    def wide_product(dv):
+        gu_own[dv, :, gate_at] = dot(x_ref[dv, :, 0:HALF], wg[...])
+        exchange[dv][0].start()
+        gu_own[dv, :, up_at] = dot(x_ref[dv, :, 0:HALF], wu[...])
+        exchange[dv][1].start()
+
+    def low_product(dv):
         low_a = dot(x_ref[dv, :, 0:QUARTER], t_ref[...])
         low_b = dot(x_ref[dv, :, QUARTER:HALF], t_ref[...])
-        gu_own[dv, :, 2 * HID :] = low_a + pltpu.roll(low_b, 64, 1)
-        exchange[dv].start()
-
-    def second_product(dv):
-        exchange[dv].wait_recv()
-        low = (gu_own[dv, :, 2 * HID :] + gu_got[dv, :, 2 * HID :]).astype(BF)
+        gu_own[dv, :, low_at] = low_a + pltpu.roll(low_b, 64, 1)
+        exchange[dv][2].start()
+
+    def second_product(dv, after=None):
+        exchange[dv][2].wait_recv()
+        low = (gu_own[dv, :, low_at] + gu_got[dv, :, low_at]).astype(BF)
         extra = dot(low, bpad[...])
-        gate = gu_own[dv, :, 0:HID] + gu_got[dv, :, 0:HID] + extra[:, 0:HID]
-        up = gu_own[dv, :, HID : 2 * HID] + gu_got[dv, :, HID : 2 * HID] + extra[:, HID:]
-        hidden = (gate / (1.0 + jnp.exp(-gate)) * up).astype(BF)
+        exchange[dv][0].wait_recv()
+        gate = gu_own[dv, :, gate_at] + gu_got[dv, :, gate_at] + extra[:, 0:HID]
+        silu = gate / (1.0 + jnp.exp(-gate))
+        exchange[dv][1].wait_recv()
+        up = gu_own[dv, :, up_at] + gu_got[dv, :, up_at] + extra[:, HID:]
+        hidden = (silu * up).astype(BF)
         narrow = dot_nt(hidden, epad[...])
         head = narrow.astype(BF).astype(F32)
         rest = narrow - head
@@ -381,24 +392,50 @@
         shares = x_ref[dv, :, HALF:WIDE].astype(F32)
         share = jnp.sum(jnp.where(picks, shares, 0.0), axis=1, keepdims=True)
         for h in range(2):
-            keep = (lane128 // 64) == h
-            thin = jnp.where(keep, split, 0.0).astype(BF)
-
-            def tile(i, carry):
-                at = pl.multiple_of(i * HID, HID)
-                there = pl.multiple_of(h * QUARTER + i * HID, HID)
-                value = dot(hidden, wd[:, pl.ds(there, HID)]) + dot(thin, ct[:, pl.ds(at, HID)])
-                p_ref[dv, :, pl.ds(there, HID)] = (value * share).astype(BF)
-                return carry
-
-            lax.fori_loop(0, QUARTER // HID, tile, 0)
-
-    first_product(0)
+            thin = jnp.where((lane128 // 64) == h, split, 0.0).astype(BF)
+            for i in range(QUARTER // HID):
+                at = i * HID
+                there = h * QUARTER + at
+                value = dot(hidden, wd[:, there : there + HID]) + dot(thin, ct[:, at : at + HID])
+                p_ref[dv, :, there : there + HID] = (value * share).astype(BF)
+            if after is not None:
+                after(h)
+
+    load_wg.wait()
+    load_wu.wait()
+    wide_product(0)
+
+    t_p.wait_recv()
+    t_fp.start()
+    t_m.wait_recv()
+    t_fm.start()
+    attend(2, 2)
+
+    for c in range(2):
+        forward(c, 3)
+    for c in range(2):
+        forward(c, 1)
+
+    t_fp.wait_recv()
+    t_fm.wait_recv()
+    for i in range(2):
+        for k in range(4):
+            block = jnp.concatenate([tx[j, k, i].astype(F32) for j in range(4)], axis=0)
+            t_ref[224 * (4 * i + k) : 224 * (4 * i + k) + 224] = block.astype(BF)
+    for k in range(14):
+        block = t_ref[128 * k : 128 * k + 128].astype(F32)
+        ct[:, 128 * k : 128 * k + 128] = block.T.astype(BF)
+    low_product(0)
+    load_wd.wait()
+    attend(4, 1)
+    second_product(0)
+
     for c in range(2):
         forward(c, 2)
-    first_product(1)
-    first_product(3)
-    second_product(0)
+    low_product(1)
+    wide_product(1)
+    low_product(3)
+    wide_product(3)
 
     a_p, a_m, b_p, b_m, c_p, c_m = [], [], [], [], [], []
     for c in range(2):
@@ -416,36 +453,30 @@
     order = (2, 1, 3, 0)
 
     second_product(1)
-    for c in range(2):
-        for du in order:
+    for du in order:
+        for c in range(2):
             b_p[c][du].start()
     second_product(3)
-    for c in range(2):
-        for du in order:
+    for du in order:
+        for c in range(2):
             b_m[c][du].start()
     for c in range(2):
         for du in range(4):
             v_fp[c][du].wait_recv()
             v_fm[c][du].wait_recv()
-    first_product(2)
-    attend(4, 1)
-    second_product(2)
-    for du in order:
-        for c in range(2):
-            a_p[c][du].start()
-            a_m[c][du].start()
+    low_product(2)
+    wide_product(2)
+
+    def begin_return(h):
+        for du in order:
+            for c in range(2):
+                (a_p, a_m)[h][c][du].start()
+
+    second_product(2, begin_return)
     attend(5, 3)
     store_att = local(att_buf, att_hbm.at[0])
 
-    for copy in z_copies + [bq_copy, e_copy] + piece_copies + [t_p, t_m, t_fp, t_fm]:
-        copy.wait_send()
-    for c in range(2):
-        for copy in [u_p[c], u_m[c], u_fp[c], u_fm[c]] + v_p[c] + v_m[c] + v_fp[c] + v_fm[c]:
-            copy.wait_send()
-    for copy in exchange:
-        copy.wait_send()
-
-    for du in order:
+    def carry_v(du):
         for c in range(2):
             r = rows_of(c, du)
             a_p[c][du].wait_recv()
@@ -472,16 +503,30 @@
         b2m.append(remote(q_sum.at[r3, left], from_right2.at[c, :, left], d["um"]))
         c2p.append(remote(q_sum.at[r1, left], from_left2.at[c, :, left], d["up"]))
         c2m.append(remote(q_sum.at[r3, right], from_right2.at[c, :, right], d["um"]))
+    carry_v(2)
+    carry_v(1)
     for c in range(2):
         gather_v(c, 2)
         a2p[c].start()
         a2m[c].start()
+    carry_v(3)
     for c in range(2):
         gather_v(c, 1)
         b2p[c].start()
+    carry_v(0)
     for c in range(2):
         gather_v(c, 3)
         b2m[c].start()
+
+    for copy in z_copies + [bq_copy, e_copy] + y_copies + t_copies + [t_p, t_m, t_fp, t_fm]:
+        copy.wait_send()
+    for c in range(2):
+        for copy in [u_p[c], u_m[c], u_fp[c], u_fm[c]] + v_p[c] + v_m[c] + v_fp[c] + v_fm[c]:
+            copy.wait_send()
+    for dv in range(4):
+        for copy in exchange[dv]:
+            copy.wait_send()
+
     for c in range(2):
         r1, r3 = rows_of(c, 1), rows_of(c, 3)
         a2p[c].wait_recv()
@@ -493,7 +538,7 @@
     for c in range(2):
         gather_v(c, 0)
 
-    z_back = [remote(z_send.at[slot], z_got.at[MIRROR[slot]], across(STEPS[slot], 0)) for slot in range(4)]
+    z_back = [remote(z_send.at[slot], z_got.at[MIRROR[slot]], across(STEPS[slot])) for slot in range(4)]
     for c in range(2):
         for copy in (b2p[c], c2p[c], b2m[c], c2m[c]):
             copy.wait_recv()
@@ -516,13 +561,26 @@
     store_att.wait()
     for copy in z_back:
         copy.wait_recv()
-    result = z_got[0].astype(F32) + z_got[1].astype(F32) + z_got[2].astype(F32) + z_got[3].astype(F32)
-    out_buf[...] = result.astype(BF)
-    store_out = local(out_buf, expert_hbm.at[0])
     for copy in z_back:
         copy.wait_send()
-    store_out.wait()
     assert count[0] == N_COPIES, count[0]
+
+
+def finish(z_got, att_in, expert_hbm, att_hbm, parts, out_buf, att_buf, sems):
+    load = pltpu.make_async_copy(z_got, parts, sems.at[0])
+    load.start()
+    load_att = pltpu.make_async_copy(att_in, att_buf, sems.at[1])
+    load_att.start()
+    load.wait()
+    total = parts[0].astype(F32) + parts[1].astype(F32) + parts[2].astype(F32) + parts[3].astype(F32)
+    out_buf[...] = total.astype(BF)
+    store = pltpu.make_async_copy(out_buf, expert_hbm.at[0], sems.at[2])
+    store.start()
+    load_att.wait()
+    store_att = pltpu.make_async_copy(att_buf, att_hbm, sems.at[3])
+    store_att.start()
+    store.wait()
+    store_att.wait()
 
 
 def body(
@@ -541,10 +599,10 @@
     adapter_down_input,
 ):
     vmem = pltpu.VMEM
-    expert_out, attention_out = pl.pallas_call(
+    returned, attended = pl.pallas_call(
         kernel,
         out_shape=(
-            jax.ShapeDtypeStruct((1, SEQ, HALF), BF),
+            jax.ShapeDtypeStruct((4, SEQ, HALF), BF),
             jax.ShapeDtypeStruct((1, SEQ, HEADS, LAT), BF),
         ),
         in_specs=[pl.BlockSpec(memory_space=pl.ANY)] * 13,
@@ -564,8 +622,6 @@
             vmem((2, 16, HALF), BF),
             vmem((2, 16, HALF), BF),
             vmem((4, SEQ, HALF), BF),
-            vmem((4, SEQ, HALF), BF),
-            vmem((SEQ, HALF), BF),
             vmem((HALF, HID), BF),
             vmem((HALF, HID), BF),
             vmem((HID, HALF), BF),
@@ -574,8 +630,9 @@
             vmem((32, HID), BF),
             vmem((16, HID), BF),
             vmem((16, SLICE, 128), BF),
-            vmem((16, SLICE, 128), BF),
-            vmem((4, 8, SLICE, 128), BF),
+            vmem((4, 4, SLICE, 128), BF),
+            vmem((4, 2, SLICE, 128), BF),
+            vmem((4, 4, 2, SLICE, 128), BF),
             vmem((QUARTER, 128), BF),
             vmem((128, QUARTER), BF),
             vmem((128, 2 * HID), BF),
@@ -608,7 +665,21 @@
         adapter_up_output,
         adapter_down_input,
     )
-    return (expert_out, attention_out)
+    return pl.pallas_call(
+        finish,
+        out_shape=(
+            jax.ShapeDtypeStruct((1, SEQ, HALF), BF),
+            jax.ShapeDtypeStruct((1, SEQ, HEADS, LAT), BF),
+        ),
+        in_specs=[pl.BlockSpec(memory_space=pltpu.HBM)] * 2,
+        out_specs=[pl.BlockSpec(memory_space=pltpu.HBM)] * 2,
+        scratch_shapes=[
+            vmem((4, SEQ, HALF), BF),
+            vmem((SEQ, HALF), BF),
+            vmem((1, SEQ, HEADS, LAT), BF),
+            pltpu.SemaphoreType.DMA((4,)),
+        ],
+    )(returned, attended)
 
 
 def solution(mesh):

time: 91.2 us -> 79.7 us (0.87); the launches traced: 89.5 us -> 79.2 us
  Pallas kernels: 85.5 us -> 78.6 us
  local copies, waits for them, and re-layouts: 3.31 us -> 0 us
    pallas_call x1 -> x2, Pallas kernels: 85.5 us -> 78.6 us  [the longest x1 76.6 us: body(): pl.pallas_call(kernel, out_shape=(jax.ShapeDtypeStruct((4, SEQ, HALF), BF...]
    unnamed x2 -> x0, local copies, waits for them, and re-layouts: 3.31 us -> none
where the time goes in v2:
time: 79.7 us; the launch traced here: 79.2 us
  Pallas kernels  78.6 us (99%)
    pallas_call x1, Pallas kernels, body(): pl.pallas_call(kernel, out_shape=(jax.ShapeDtypeStruct((4, SEQ, HALF), BF...  76.6 us
    pallas_call x1, Pallas kernels, body(): pl.pallas_call(finish, out_shape=(jax.ShapeDtypeStruct((1, SEQ, HALF), BF...  1.99 us

profile of v2, /device:TPU:8, one launch (start us, length us, event | category | flops | bytes accessed | tf_op | source)
XLA Modules:
  0.0 79.2 jit_solution(8630770031537277119)
XLA Ops:
  0.6 76.6 %shard_map.140 = (bf16[4,8,3584]{2,1,0:T(8,128)(2,1)}, bf16[1,8,64,512]{3,2,1,0:T(8,128)(2,1)}) custom-call(bf16[1,8,64,576]{3,2,1,0:T(8,128)(2,1)} %q_hbm.1, bf16[1,8,576,512]{3,2,1,0:T(8,128)(2,1)} %bitcast.1, s32[1,8]{1,0:T(1,128)} %len_hbm.1, bf16[1,8,3584]{2,1,0:T(8,128)(2,1)} %rows_hbm.1, s32[1,8,8]{2,1,0:T(8,128)} %ids_hbm.1, f32[1,8,8]{2,1,0:T(8,128)} %gates_hbm.1, ...), custom_call_target="tpu_custom_call" | custom-call | tf_op jit(solution)/shard_map/pallas_call | solution.py:602
  77.2 2.0 %shard_map.141 = (bf16[1,8,3584]{2,1,0:T(8,128)(2,1)}, bf16[1,8,64,512]{3,2,1,0:T(8,128)(2,1)}) custom-call(bf16[4,8,3584]{2,1,0:T(8,128)(2,1)} %get-tuple-element.4.z_got, bf16[1,8,64,512]{3,2,1,0:T(8,128)(2,1)} %get-tuple-element.5.att_in), custom_call_target="tpu_custom_call" | custom-call | tf_op jit(solution)/shard_map/pallas_call | solution.py:668

commit v3 on v2

--- a/solution.py
+++ b/solution.py
@@ -178,35 +178,34 @@
     load_ain.wait()
     load_cout.wait()
     lane56 = lax.broadcasted_iota(jnp.int32, (SLICE, 128), 1)
-    shift = (y // 2) * 64
-    mine = (lane56 >= shift) & (lane56 < shift + 64)
-    place = lane56 % 64
-    for e in range(16):
+
+    def turned(tile, by):
+        by = by % 128
+        return tile if by == 0 else pltpu.roll(tile, by, 1)
+
+    def piece(e, at):
         a_tile = ain[:, 128 * (e // 4) : 128 * (e // 4) + 128].astype(F32)
         c_tile = cout[:, 128 * (e // 8) : 128 * (e // 8) + 128].astype(F32)
-        a_at, c_at = 32 * (e % 4), 16 * (e % 8)
-
-        def turned(tile, by):
-            by = by % 128
-            return tile if by == 0 else pltpu.roll(tile, by, 1)
-
-        low = jnp.where(
-            place < 32,
-            turned(a_tile, -a_at),
-            jnp.where(place < 48, turned(c_tile, 32 - c_at), turned(c_tile, 48 - c_at)),
+        c_from = at - 16 * (e % 8)
+        return jnp.where(
+            lane56 < at + 32,
+            turned(a_tile, at - 32 * (e % 4)),
+            jnp.where(lane56 < at + 48, turned(c_tile, 32 + c_from), turned(c_tile, 48 + c_from)),
         )
-        low = jnp.where(lane56 < 64, low, 0.0)
-        both = low + pltpu.roll(low, 64, 1)
-        pieces[e] = jnp.where(mine, both, 0.0).astype(BF)
+
+    for i in range(4):
+        for k in range(2):
+            tile = jnp.where(lane56 < 64, piece(4 * i + k, 0), piece(4 * i + k + 2, 64))
+            pieces[i, k] = tile.astype(BF)
     y_copies = [
         remote(
-            pieces.at[pl.ds(((y + dy) % 4) * 4, 4)], pieces_got.at[y], plane(dy, 0)
+            pieces.at[(y + dy) % 4], pieces_got.at[y], plane(dy, 0)
         )
         for dy in (1, 3, 2)
     ]
     for copy in y_copies:
         copy.start()
-    pieces_got[y] = pieces[pl.ds(y * 4, 4)]
+    pieces_got[y] = pieces[y]
 
     def attend(first_seq, n):
         def one(s, carry):
@@ -227,7 +226,7 @@
         lax.fori_loop(first_seq, first_seq + n, one, 0)
 
     def rows_of(chain, du):
-        return pl.ds((chain * 4 + du) * 16, 16)
+        return pl.ds(((0, 2, 3, 1)[du] * 2 + chain) * 16, 16)
 
     along = [
         dict(up=plane(0, 1), um=plane(0, 3), vp=plane(1, 0), vm=plane(3, 0)),
@@ -294,7 +293,6 @@
         u_m[c].wait_recv()
         u_fm[c].start()
         spread(c, 3)
-        spread(c, 1)
 
     def turn_far(c):
         u_fp[c].wait_recv()
@@ -307,8 +305,13 @@
         copy.wait_recv()
     for k in range(4):
         for i in range(2):
-            both = pieces_got[i, k].astype(F32) + pieces_got[i + 2, k].astype(F32)
-            joined[k, i] = both.astype(BF)
+            low = pieces_got[i, k % 2].astype(F32)
+            high = pieces_got[i + 2, k % 2].astype(F32)
+            if k < 2:
+                high = pltpu.roll(high, 64, 1)
+            else:
+                low = pltpu.roll(low, 64, 1)
+            joined[k, i] = jnp.where(lane56 < 64, low, high).astype(BF)
     t_copies = [
         remote(joined.at[((z + step + 8) % 8) // 2], tx.at[x, zh], across(step)) for step in STEPS
     ]
@@ -321,8 +324,7 @@
     load_cache.wait()
     attend(0, 1)
     turn(0)
-    attend(1, 1)
-    turn(1)
+    forward(0, 0)
 
     for copy in t_copies:
         copy.wait_recv()
@@ -334,10 +336,10 @@
     t_p.start()
     t_m.start()
 
-    forward(0, 0)
-    turn_far(0)
+    turn(1)
+    spread(0, 1)
+    spread(1, 1)
     forward(1, 0)
-    turn_far(1)
 
     bq_copy.wait_recv()
     e_copy.wait_recv()
@@ -347,6 +349,13 @@
     epad[...] = jnp.zeros_like(epad)
     for at in (32, 48, 96, 112):
         epad[at : at + 16] = e_got[...]
+
+    turn_far(0)
+    turn_far(1)
+    t_p.wait_recv()
+    t_fp.start()
+    t_m.wait_recv()
+    t_fm.start()
 
     lane128 = lax.broadcasted_iota(jnp.int32, (128, 128), 1)
     low_at, gate_at, up_at = (
@@ -362,34 +371,40 @@
         for dv in range(4)
     ]
 
-    def wide_product(dv):
-        gu_own[dv, :, gate_at] = dot(x_ref[dv, :, 0:HALF], wg[...])
-        exchange[dv][0].start()
-        gu_own[dv, :, up_at] = dot(x_ref[dv, :, 0:HALF], wu[...])
-        exchange[dv][1].start()
-
-    def low_product(dv):
-        low_a = dot(x_ref[dv, :, 0:QUARTER], t_ref[...])
-        low_b = dot(x_ref[dv, :, QUARTER:HALF], t_ref[...])
-        gu_own[dv, :, low_at] = low_a + pltpu.roll(low_b, 64, 1)
-        exchange[dv][2].start()
-
-    def second_product(dv, after=None):
-        exchange[dv][2].wait_recv()
-        low = (gu_own[dv, :, low_at] + gu_got[dv, :, low_at]).astype(BF)
+    groups = (((0, 0, 128),), ((1, 0, 64), (3, 0, 64)), ((1, 64, 64), (3, 64, 64)), ((2, 0, 128),))
+
+    def rows_in(g, lo, hi):
+        parts = [x_ref[dv, at : at + n, lo:hi] for dv, at, n in groups[g]]
+        return parts[0] if len(parts) == 1 else jnp.concatenate(parts, axis=0)
+
+    def wide_product(g):
+        gu_own[g, :, gate_at] = dot(rows_in(g, 0, HALF), wg[...])
+        exchange[g][0].start()
+        gu_own[g, :, up_at] = dot(rows_in(g, 0, HALF), wu[...])
+        exchange[g][1].start()
+
+    def low_product(g):
+        low_a = dot(rows_in(g, 0, QUARTER), t_ref[...])
+        low_b = dot(rows_in(g, QUARTER, HALF), t_ref[...])
+        gu_own[g, :, low_at] = low_a + pltpu.roll(low_b, 64, 1)
+        exchange[g][2].start()
+
+    def second_product(g, after=None):
+        exchange[g][2].wait_recv()
+        low = (gu_own[g, :, low_at] + gu_got[g, :, low_at]).astype(BF)
         extra = dot(low, bpad[...])
-        exchange[dv][0].wait_recv()
-        gate = gu_own[dv, :, gate_at] + gu_got[dv, :, gate_at] + extra[:, 0:HID]
+        exchange[g][0].wait_recv()
+        gate = gu_own[g, :, gate_at] + gu_got[g, :, gate_at] + extra[:, 0:HID]
         silu = gate / (1.0 + jnp.exp(-gate))
-        exchange[dv][1].wait_recv()
-        up = gu_own[dv, :, up_at] + gu_got[dv, :, up_at] + extra[:, HID:]
+        exchange[g][1].wait_recv()
+        up = gu_own[g, :, up_at] + gu_got[g, :, up_at] + extra[:, HID:]
         hidden = (silu * up).astype(BF)
         narrow = dot_nt(hidden, epad[...])
         head = narrow.astype(BF).astype(F32)
         rest = narrow - head
         split = jnp.where((lane128 % 64) < 48, head, rest)
         picks = (lane128 % 32 == expert) & (lane128 < 96)
-        shares = x_ref[dv, :, HALF:WIDE].astype(F32)
+        shares = rows_in(g, HALF, WIDE).astype(F32)
         share = jnp.sum(jnp.where(picks, shares, 0.0), axis=1, keepdims=True)
         for h in range(2):
             thin = jnp.where((lane128 // 64) == h, split, 0.0).astype(BF)
@@ -397,24 +412,25 @@
                 at = i * HID
                 there = h * QUARTER + at
                 value = dot(hidden, wd[:, there : there + HID]) + dot(thin, ct[:, at : at + HID])
-                p_ref[dv, :, there : there + HID] = (value * share).astype(BF)
+                value = (value * share).astype(BF)
+                done = 0
+                for dv, begin, n in groups[g]:
+                    p_ref[dv, begin : begin + n, there : there + HID] = value[done : done + n]
+                    done += n
             if after is not None:
                 after(h)
 
     load_wg.wait()
     load_wu.wait()
     wide_product(0)
-
-    t_p.wait_recv()
-    t_fp.start()
-    t_m.wait_recv()
-    t_fm.start()
-    attend(2, 2)
-
-    for c in range(2):
-        forward(c, 3)
-    for c in range(2):
-        forward(c, 1)
+    forward(0, 3)
+    forward(1, 3)
+    wide_product(1)
+    forward(0, 1)
+    forward(1, 1)
+    forward(0, 2)
+    forward(1, 2)
+    wide_product(2)
 
     t_fp.wait_recv()
     t_fm.wait_recv()
@@ -425,17 +441,10 @@
     for k in range(14):
         block = t_ref[128 * k : 128 * k + 128].astype(F32)
         ct[:, 128 * k : 128 * k + 128] = block.T.astype(BF)
-    low_product(0)
+    low_product(1)
+    low_product(2)
     load_wd.wait()
-    attend(4, 1)
-    second_product(0)
-
-    for c in range(2):
-        forward(c, 2)
-    low_product(1)
-    wide_product(1)
-    low_product(3)
-    wide_product(3)
+    second_product(1)
 
     a_p, a_m, b_p, b_m, c_p, c_m = [], [], [], [], [], []
     for c in range(2):
@@ -452,39 +461,42 @@
             c_m[c].append(remote(p_ref.at[3, r, right], from_right.at[r, right], d["vm"]))
     order = (2, 1, 3, 0)
 
-    second_product(1)
-    for du in order:
+    def direct(du):
         for c in range(2):
             b_p[c][du].start()
-    second_product(3)
-    for du in order:
-        for c in range(2):
             b_m[c][du].start()
+
+    direct(3)
+    direct(0)
+    second_product(2)
+    direct(2)
+    direct(1)
     for c in range(2):
         for du in range(4):
             v_fp[c][du].wait_recv()
             v_fm[c][du].wait_recv()
-    low_product(2)
-    wide_product(2)
+    low_product(3)
+    wide_product(3)
+    low_product(0)
 
     def begin_return(h):
         for du in order:
-            for c in range(2):
+            for c in (1, 0):
                 (a_p, a_m)[h][c][du].start()
 
-    second_product(2, begin_return)
-    attend(5, 3)
+    second_product(3, begin_return)
+    second_product(0)
+    attend(1, 7)
     store_att = local(att_buf, att_hbm.at[0])
 
-    def carry_v(du):
-        for c in range(2):
-            r = rows_of(c, du)
-            a_p[c][du].wait_recv()
-            p_ref[1, r, left] = (p_ref[1, r, left].astype(F32) + ra[0, r].astype(F32)).astype(BF)
-            c_p[c][du].start()
-            a_m[c][du].wait_recv()
-            p_ref[3, r, right] = (p_ref[3, r, right].astype(F32) + ra[1, r].astype(F32)).astype(BF)
-            c_m[c][du].start()
+    def carry_v(c, du):
+        r = rows_of(c, du)
+        a_p[c][du].wait_recv()
+        p_ref[1, r, left] = (p_ref[1, r, left].astype(F32) + ra[0, r].astype(F32)).astype(BF)
+        c_p[c][du].start()
+        a_m[c][du].wait_recv()
+        p_ref[3, r, right] = (p_ref[3, r, right].astype(F32) + ra[1, r].astype(F32)).astype(BF)
+        c_m[c][du].start()
 
     def gather_v(c, du):
         r = rows_of(c, du)
@@ -503,31 +515,16 @@
         b2m.append(remote(q_sum.at[r3, left], from_right2.at[c, :, left], d["um"]))
         c2p.append(remote(q_sum.at[r1, left], from_left2.at[c, :, left], d["up"]))
         c2m.append(remote(q_sum.at[r3, right], from_right2.at[c, :, right], d["um"]))
-    carry_v(2)
-    carry_v(1)
-    for c in range(2):
+    def turn_back(c):
         gather_v(c, 2)
         a2p[c].start()
         a2m[c].start()
-    carry_v(3)
-    for c in range(2):
-        gather_v(c, 1)
-        b2p[c].start()
-    carry_v(0)
-    for c in range(2):
-        gather_v(c, 3)
-        b2m[c].start()
-
-    for copy in z_copies + [bq_copy, e_copy] + y_copies + t_copies + [t_p, t_m, t_fp, t_fm]:
-        copy.wait_send()
-    for c in range(2):
-        for copy in [u_p[c], u_m[c], u_fp[c], u_fm[c]] + v_p[c] + v_m[c] + v_fp[c] + v_fm[c]:
-            copy.wait_send()
-    for dv in range(4):
-        for copy in exchange[dv]:
-            copy.wait_send()
-
-    for c in range(2):
+
+    def near_back(c, du):
+        gather_v(c, du)
+        (b2p if du == 1 else b2m)[c].start()
+
+    def carry_u(c):
         r1, r3 = rows_of(c, 1), rows_of(c, 3)
         a2p[c].wait_recv()
         q_sum[r1, left] = (q_sum[r1, left].astype(F32) + ra2[0, c].astype(F32)).astype(BF)
@@ -535,11 +532,12 @@
         a2m[c].wait_recv()
         q_sum[r3, right] = (q_sum[r3, right].astype(F32) + ra2[1, c].astype(F32)).astype(BF)
         c2m[c].start()
-    for c in range(2):
-        gather_v(c, 0)
-
-    z_back = [remote(z_send.at[slot], z_got.at[MIRROR[slot]], across(STEPS[slot])) for slot in range(4)]
-    for c in range(2):
+
+    z_back = [
+        remote(z_send.at[slot], z_got.at[MIRROR[slot]], across(STEPS[slot])) for slot in range(4)
+    ]
+
+    def cross_back(c):
         for copy in (b2p[c], c2p[c], b2m[c], c2m[c]):
             copy.wait_recv()
         total = (
@@ -551,6 +549,36 @@
             slot = CHAIN_SLOTS[c][i]
             z_send[slot] = total[8 * i : 8 * i + 8].astype(BF)
             z_back[slot].start()
+
+    carry_v(1, 2)
+    carry_v(0, 2)
+    carry_v(1, 1)
+    carry_v(0, 1)
+    turn_back(1)
+    carry_v(1, 3)
+    near_back(1, 1)
+    carry_v(1, 0)
+    near_back(1, 3)
+    carry_v(0, 3)
+    carry_u(1)
+    carry_v(0, 0)
+    turn_back(0)
+    gather_v(1, 0)
+    near_back(0, 1)
+    near_back(0, 3)
+    cross_back(1)
+    carry_u(0)
+    gather_v(0, 0)
+    cross_back(0)
+
+    for copy in z_copies + [bq_copy, e_copy] + y_copies + t_copies + [t_p, t_m, t_fp, t_fm]:
+        copy.wait_send()
+    for c in range(2):
+        for copy in [u_p[c], u_m[c], u_fp[c], u_fm[c]] + v_p[c] + v_m[c] + v_fp[c] + v_fm[c]:
+            copy.wait_send()
+    for g in range(4):
+        for copy in exchange[g]:
+            copy.wait_send()
 
     for c in range(2):
         for group in (a_p, a_m, b_p, b_m, c_p, c_m):
@@ -629,8 +657,8 @@
             vmem((SLICE, 256), BF),
             vmem((32, HID), BF),
             vmem((16, HID), BF),
-            vmem((16, SLICE, 128), BF),
-            vmem((4, 4, SLICE, 128), BF),
+            vmem((4, 2, SLICE, 128), BF),
+            vmem((4, 2, SLICE, 128), BF),
             vmem((4, 2, SLICE, 128), BF),
             vmem((4, 4, 2, SLICE, 128), BF),
             vmem((QUARTER, 128), BF),

time: 79.7 us -> 74.4 us (0.934)
  Pallas kernels: 78.6 us -> 73.7 us
    pallas_call x1, Pallas kernels: 76.6 us -> 71.7 us  [body(): pl.pallas_call(kernel, out_shape=(jax.ShapeDtypeStruct((4, SEQ, HALF), BF...]
where the time goes in v3:
time: 74.4 us; the launch traced here: 74.3 us
  Pallas kernels  73.7 us (99%)
    pallas_call x1, Pallas kernels, body(): pl.pallas_call(kernel, out_shape=(jax.ShapeDtypeStruct((4, SEQ, HALF), BF...  71.7 us
    pallas_call x1, Pallas kernels, body(): pl.pallas_call(finish, out_shape=(jax.ShapeDtypeStruct((1, SEQ, HALF), BF...  1.99 us

profile of v3, /device:TPU:8, one launch (start us, length us, event | category | flops | bytes accessed | tf_op | source)
XLA Modules:
  0.0 74.3 jit_solution(1692963296287165004)
XLA Ops:
  0.6 71.7 %shard_map.140 = (bf16[4,8,3584]{2,1,0:T(8,128)(2,1)}, bf16[1,8,64,512]{3,2,1,0:T(8,128)(2,1)}) custom-call(bf16[1,8,64,576]{3,2,1,0:T(8,128)(2,1)} %q_hbm.1, bf16[1,8,576,512]{3,2,1,0:T(8,128)(2,1)} %bitcast.1, s32[1,8]{1,0:T(1,128)} %len_hbm.1, bf16[1,8,3584]{2,1,0:T(8,128)(2,1)} %rows_hbm.1, s32[1,8,8]{2,1,0:T(8,128)} %ids_hbm.1, f32[1,8,8]{2,1,0:T(8,128)} %gates_hbm.1, ...), custom_call_target="tpu_custom_call" | custom-call | tf_op jit(solution)/shard_map/pallas_call | solution.py:630
  72.3 2.0 %shard_map.141 = (bf16[1,8,3584]{2,1,0:T(8,128)(2,1)}, bf16[1,8,64,512]{3,2,1,0:T(8,128)(2,1)}) custom-call(bf16[4,8,3584]{2,1,0:T(8,128)(2,1)} %get-tuple-element.4.z_got, bf16[1,8,64,512]{3,2,1,0:T(8,128)(2,1)} %get-tuple-element.5.att_in), custom_call_target="tpu_custom_call" | custom-call | tf_op jit(solution)/shard_map/pallas_call | solution.py:696

commit v4 on v3

--- a/solution.py
+++ b/solution.py
@@ -168,8 +168,8 @@
     z_copies = [
         remote(unit, zbuf.at[MIRROR[slot]], across(STEPS[slot])) for slot in range(4)
     ]
-    for copy in z_copies:
-        copy.start()
+    z_copies[0].start()
+    z_copies[1].start()
     bq_copy = remote(bq_hbm.at[0], bq_got, partner)
     e_copy = remote(e_hbm.at[0], e_got, partner)
     bq_copy.start()
@@ -197,6 +197,8 @@
         for k in range(2):
             tile = jnp.where(lane56 < 64, piece(4 * i + k, 0), piece(4 * i + k + 2, 64))
             pieces[i, k] = tile.astype(BF)
+    z_copies[2].start()
+    z_copies[3].start()
     y_copies = [
         remote(
             pieces.at[(y + dy) % 4], pieces_got.at[y], plane(dy, 0)
@@ -524,11 +526,14 @@
         gather_v(c, du)
         (b2p if du == 1 else b2m)[c].start()
 
-    def carry_u(c):
-        r1, r3 = rows_of(c, 1), rows_of(c, 3)
+    def carry_up(c):
+        r1 = rows_of(c, 1)
         a2p[c].wait_recv()
         q_sum[r1, left] = (q_sum[r1, left].astype(F32) + ra2[0, c].astype(F32)).astype(BF)
         c2p[c].start()
+
+    def carry_um(c):
+        r3 = rows_of(c, 3)
         a2m[c].wait_recv()
         q_sum[r3, right] = (q_sum[r3, right].astype(F32) + ra2[1, c].astype(F32)).astype(BF)
         c2m[c].start()
@@ -550,26 +555,27 @@
             z_send[slot] = total[8 * i : 8 * i + 8].astype(BF)
             z_back[slot].start()
 
-    carry_v(1, 2)
-    carry_v(0, 2)
-    carry_v(1, 1)
-    carry_v(0, 1)
-    turn_back(1)
-    carry_v(1, 3)
-    near_back(1, 1)
-    carry_v(1, 0)
-    near_back(1, 3)
-    carry_v(0, 3)
-    carry_u(1)
-    carry_v(0, 0)
-    turn_back(0)
-    gather_v(1, 0)
-    near_back(0, 1)
-    near_back(0, 3)
-    cross_back(1)
-    carry_u(0)
-    gather_v(0, 0)
-    cross_back(0)
+    both = (1, 0)
+    for du in (2, 1):
+        for c in both:
+            carry_v(c, du)
+    for c in both:
+        turn_back(c)
+    for c in both:
+        carry_v(c, 3)
+    for c in both:
+        near_back(c, 1)
+    for c in both:
+        carry_v(c, 0)
+    for c in both:
+        carry_up(c)
+    for c in both:
+        near_back(c, 3)
+        carry_um(c)
+    for c in both:
+        gather_v(c, 0)
+    for c in both:
+        cross_back(c)
 
     for copy in z_copies + [bq_copy, e_copy] + y_copies + t_copies + [t_p, t_m, t_fp, t_fm]:
         copy.wait_send()

time: 74.4 us -> 73.4 us (0.987)
  Pallas kernels: 73.7 us -> 72.6 us
    pallas_call x1, Pallas kernels: 71.7 us -> 70.6 us  [body(): pl.pallas_call(kernel, out_shape=(jax.ShapeDtypeStruct((4, SEQ, HALF), BF...]
where the time goes in v4:
time: 73.4 us; the launch traced here: 73.2 us
  Pallas kernels  72.6 us (99%)
    pallas_call x1, Pallas kernels, body(): pl.pallas_call(kernel, out_shape=(jax.ShapeDtypeStruct((4, SEQ, HALF), BF...  70.6 us
    pallas_call x1, Pallas kernels, body(): pl.pallas_call(finish, out_shape=(jax.ShapeDtypeStruct((1, SEQ, HALF), BF...  1.99 us

profile of v4, /device:TPU:8, one launch (start us, length us, event | category | flops | bytes accessed | tf_op | source)
XLA Modules:
  0.0 73.2 jit_solution(4047325366978442968)
XLA Ops:
  0.6 70.6 %shard_map.140 = (bf16[4,8,3584]{2,1,0:T(8,128)(2,1)}, bf16[1,8,64,512]{3,2,1,0:T(8,128)(2,1)}) custom-call(bf16[1,8,64,576]{3,2,1,0:T(8,128)(2,1)} %q_hbm.1, bf16[1,8,576,512]{3,2,1,0:T(8,128)(2,1)} %bitcast.1, s32[1,8]{1,0:T(1,128)} %len_hbm.1, bf16[1,8,3584]{2,1,0:T(8,128)(2,1)} %rows_hbm.1, s32[1,8,8]{2,1,0:T(8,128)} %ids_hbm.1, f32[1,8,8]{2,1,0:T(8,128)} %gates_hbm.1, ...), custom_call_target="tpu_custom_call" | custom-call | tf_op jit(solution)/shard_map/pallas_call | solution.py:636
  71.3 2.0 %shard_map.141 = (bf16[1,8,3584]{2,1,0:T(8,128)(2,1)}, bf16[1,8,64,512]{3,2,1,0:T(8,128)(2,1)}) custom-call(bf16[4,8,3584]{2,1,0:T(8,128)(2,1)} %get-tuple-element.4.z_got, bf16[1,8,64,512]{3,2,1,0:T(8,128)(2,1)} %get-tuple-element.5.att_in), custom_call_target="tpu_custom_call" | custom-call | tf_op jit(solution)/shard_map/pallas_call | solution.py:702
